TPU v7x, 128 devices: a whole 4x4x4 slice. The times are simulated.
128 devices in a mesh: ex: 8 (over x, core), qry: 16 (over y, z).
Axes of the slice: x: 4, y: 4, z: 4, core: 2. Of those that a mesh axis runs over, the one named last changes fastest.
Arguments:
- train_proj: bfloat16 [16384, 4096], P('ex', 'qry'), may hold values from -6 to 6
- query_proj: bfloat16 [8192, 4096], P('qry', 'ex'), may hold values from -0.09375 to 0.09375
- out_weight: float32 [16384], P('ex'), may hold values from 0.1 to 1
- train_feat: float32 [16384, 16384], P('qry', 'ex'), may hold values from -6 to 6
- query_feat: float32 [8192, 16384], P('qry', 'ex'), may hold values from -0.046875 to 0.046875
- candidates: int32 [64, 2], replicated, may hold values from 0 to 127, as said below
Outputs:
- scores: float32 [16384, 8192], P('ex', 'qry')
- exact: float32 [64, 2, 128, 128], P('qry', None, 'ex')
Inputs may be any that keep to these rules, and one draw needn't show every extreme that they name: `candidates`: split the training rows into equal ranges, one for each qry index in order. The 8 entries of the tiles of one qry index name blocks in pairwise different ranges; some ranges are named far more often than others.
All inputs are finite; a program needn't handle non-finite values.
Results may differ from a plain program's by a relative error of at most 0.0003.
Values may be sent and summed in bfloat16 or wider, within the bound.
A program may use at most 192 MiB of HBM per device.

v0:
```python
import jax
import jax.numpy as jnp
from jax import lax
from jax.sharding import PartitionSpec as P

BLOCK_ROWS = 128
CANDS = 2


def local(train_proj, query_proj, out_weight, train_feat, query_feat, candidates):
    queries_full = lax.all_gather(query_proj, "ex", axis=1, tiled=True)
    products = lax.dot_general(
        lax.all_gather(train_proj, "qry", axis=1, tiled=True),
        queries_full,
        (((1,), (1,)), ((), ())),
        preferred_element_type=jnp.float32,
    )
    scores = products * out_weight[:, None]
    devices = lax.axis_size("qry")
    my_index = lax.axis_index("qry")
    width = train_feat.shape[1]
    held_blocks = train_feat.shape[0] // BLOCK_ROWS
    tiles_here = query_feat.shape[0] // BLOCK_ROWS
    per_device = tiles_here * CANDS
    block_view = train_feat.reshape(held_blocks, BLOCK_ROWS, width)
    tile_view = query_feat.reshape(tiles_here, BLOCK_ROWS, width)
    items = candidates.reshape(devices, per_device)
    owner_of = items // held_blocks
    local_block = items % held_blocks
    mine = lax.dynamic_slice_in_dim(items, my_index, 1, 0)[0]
    my_owner = mine // held_blocks
    wanted_here = owner_of == my_index
    pick_block = jnp.sum(jnp.where(wanted_here, local_block, 0), axis=1)
    owner_match = my_owner[None, :] == jnp.arange(devices)[:, None]
    tile_number = jnp.arange(per_device) // CANDS
    pick_tile = jnp.sum(jnp.where(owner_match, tile_number[None, :], 0), axis=1)
    outgoing = tile_view[pick_tile]
    arrived = lax.all_to_all(outgoing, "qry", split_axis=0, concat_axis=0, tiled=True)
    own_rows = block_view[pick_block]
    results = jnp.einsum("srf,sqf->srq", own_rows, arrived, precision=lax.Precision.HIGHEST)
    returned = lax.all_to_all(results, "qry", split_axis=0, concat_axis=0, tiled=True)
    partial_value = returned[my_owner].reshape(tiles_here, CANDS, BLOCK_ROWS, BLOCK_ROWS)
    exact = lax.psum_scatter(partial_value, "ex", scatter_dimension=2, tiled=True)
    return (scores, exact)


def solution(mesh):
    placed = (P("ex", "qry"), P("qry", "ex"), P("ex"), P("qry", "ex"), P("qry", "ex"), P())
    return jax.shard_map(
        local,
        mesh=mesh,
        in_specs=placed,
        out_specs=(P("ex", "qry"), P("qry", None, "ex", None)),
        check_vma=False,
    )
```

profile of v0, /device:TPU:9, one launch (start us, length us, event | category | flops | bytes accessed | tf_op | source)
XLA Modules:
  0.0 442.3 jit_solution(17652600933228876235)
XLA Ops:
  7.2 0.0 all-gather.5.cloned.1.call-start
  7.2 0.7 all-gather.5.cloned.1.call-update
  7.9 0.0 all-gather.3.cloned.1.call-start
  7.9 0.7 all-gather.3.cloned.1.call-update
  8.7 0.8 copy.10
  9.4 0.1 reshape.138
  9.5 0.1 select_reduce_fusion
  9.6 10.1 %gather_fusion.1 = f32[16,128,2048]{2,1,0:T(8,128)} fusion(f32[4,128,2048]{2,1,0:T(8,128)} %bitcast.29, s32[1024]{0:T(1024)S(1)} %pad_clamp_fusion.1), kind=kCustom, calls=%fused_computation.1 | custom fusion | bytes 33554496 | tf_op jit(solution)/shard_map/gather | solution.py:37
  19.7 0.0 copy-start
  19.7 8.0 %all-to-all-start = ((f32[16,128,2048]{2,1,0:T(8,128)}), f32[16,128,2048]{2,1,0:T(8,128)}, u32[]{:S(2)}, u32[]{:S(2)}) async-start(f32[16,128,2048]{2,1,0:T(8,128)} %gather_fusion.1), calls=%async_computation | async-start | bytes 33554432 | tf_op jit(solution)/shard_map/all_to_all | solution.py:38
  27.7 0.0 copy-done
  27.7 0.1 reduce_sum.30
  27.8 0.1 reduce_sum.31
  28.0 11.6 %gather_fusion = f32[16,128,2048]{2,1,0:T(8,128)} fusion(f32[8,128,2048]{2,1,0:T(8,128)} %bitcast.30, s32[1024]{0:T(1024)S(1)} %pad_clamp_fusion.2), kind=kCustom, calls=%fused_computation | custom fusion | bytes 33554496 | tf_op jit(solution)/shard_map/gather | solution.py:39
  39.6 0.0 copy-start.1
  39.6 231.6 %all-to-all-done = f32[16,128,2048]{2,1,0:T(8,128)} async-done(((f32[16,128,2048]{2,1,0:T(8,128)}), f32[16,128,2048]{2,1,0:T(8,128)}, u32[]{:S(2)}, u32[]{:S(2)}) %all-to-all-start) | async-done | bytes 16777248 | tf_op jit(solution)/shard_map/all_to_all | solution.py:38
  271.2 20.3 %fusion.5 = f32[16,128,128]{2,1,0:T(8,128)} fusion(f32[16,128,2048]{2,1,0:T(8,128)} %gather_fusion, f32[16,128,2048]{2,1,0:T(8,128)} %all-to-all-done), kind=kOutput, calls=%fused_computation.37 | convolution fusion | flops 6442450944 | bytes 34603008 | tf_op jit(solution)/shard_map/srf,sqf->srq/dot_general | solution.py:40
  291.5 76.1 %all-to-all-start.1 = ((f32[16,128,128]{2,1,0:T(8,128)}), f32[16,128,128]{2,1,0:T(8,128)S(1)}, u32[]{:S(2)}, u32[]{:S(2)}) async-start(f32[16,128,128]{2,1,0:T(8,128)} %fusion.5), calls=%async_computation.1 | async-start | bytes 2097152 | tf_op jit(solution)/shard_map/all_to_all | solution.py:41
  367.5 0.0 reduce-scatter.2.cloned.1.call-start
  367.6 24.6 %all-to-all-done.1 = f32[16,128,128]{2,1,0:T(8,128)S(1)} async-done(((f32[16,128,128]{2,1,0:T(8,128)}), f32[16,128,128]{2,1,0:T(8,128)S(1)}, u32[]{:S(2)}, u32[]{:S(2)}) %all-to-all-start.1) | async-done | bytes 1048608 | tf_op jit(solution)/shard_map/all_to_all | solution.py:41
  392.2 1.4 gather_fusion.2
  393.6 0.0 reduce-scatter.2.cloned.1.call-update
  393.6 0.0 all-gather.5.cloned.1.call-done
  393.6 7.8 %all-gather.3.cloned.1.call-done = bf16[2048,4096]{1,0:T(8,128)(2,1)} async-done(((bf16[2048,256]{1,0:T(8,128)(2,1)}), bf16[2048,4096]{1,0:T(8,128)(2,1)}) %all-gather.3.cloned.1.call-update) | async-done | bytes 16777232 | tf_op jit(solution)/shard_map/all_gather | solution.py:13
  401.4 0.0 copy-done.1
  401.4 14.9 %convolution_multiply_fusion = f32[2048,512]{1,0:T(8,128)} fusion(bf16[2048,4096]{1,0:T(8,128)(2,1)} %all-gather.3.cloned.1.call-done, bf16[512,4096]{1,0:T(8,128)(2,1)} %all-gather.5.cloned.1.call-done, f32[2048]{0:T(1024)S(1)} %copy-done.1), kind=kOutput, calls=%fused_computation.3 | convolution fusion | flops 8590983168 | bytes 25174016 | tf_op jit(solution)/shard_map/dot_general | solution.py:12
  416.3 19.4 %reduce-scatter.2.cloned.1.call-done = f32[4,2,16,128]{3,2,1,0:T(8,128)} async-done(((f32[4,2,128,128]{3,2,1,0:T(8,128)}), f32[4,2,16,128]{3,2,1,0:T(8,128)}) %reduce-scatter.2.cloned.1.call-update) | async-done | bytes 65552 | tf_op jit(solution)/shard_map/reduce_scatter | solution.py:43
  (9 shorter events, 0.1 us)
Async XLA Ops:
  7.2 386.4 %all-gather.5.cloned.1.call-start = ((), (), s32[]{:S(2)}) async-start(), calls=%async_computation.4 | async-start | bytes 4718592 | tf_op jit(solution)/shard_map/all_gather | solution.py:11
  7.9 393.5 %all-gather.3.cloned.1.call-start = ((), (), s32[]{:S(2)}) async-start(), calls=%async_computation.3 | async-start | bytes 17825792 | tf_op jit(solution)/shard_map/all_gather | solution.py:13
  19.7 8.0 %copy-start = (s32[64,2]{0,1:T(2,128)S(1)}, s32[64,2]{0,1:T(2,128)}, u32[]{:S(2)}) copy-start(s32[64,2]{0,1:T(2,128)} %param.11) | copy-start | bytes 1540
  19.7 251.4 %all-to-all-start = ((f32[16,128,2048]{2,1,0:T(8,128)}), f32[16,128,2048]{2,1,0:T(8,128)}, u32[]{:S(2)}, u32[]{:S(2)}) async-start(f32[16,128,2048]{2,1,0:T(8,128)} %gather_fusion.1), calls=%async_computation | async-start | bytes 33554432 | tf_op jit(solution)/shard_map/all_to_all | solution.py:38
  39.6 361.8 %copy-start.1 = (f32[2048]{0:T(1024)S(1)}, f32[2048]{0:T(1024)}, u32[]{:S(2)}) copy-start(f32[2048]{0:T(1024)} %param.8) | copy-start | bytes 24580
  291.5 100.7 %all-to-all-start.1 = ((f32[16,128,128]{2,1,0:T(8,128)}), f32[16,128,128]{2,1,0:T(8,128)S(1)}, u32[]{:S(2)}, u32[]{:S(2)}) async-start(f32[16,128,128]{2,1,0:T(8,128)} %fusion.5), calls=%async_computation.1 | async-start | bytes 2097152 | tf_op jit(solution)/shard_map/all_to_all | solution.py:41
  367.5 68.2 %reduce-scatter.2.cloned.1.call-start = ((), (), s32[]{:S(2)}) async-start(), calls=%async_computation.5 | async-start | bytes 589824 | tf_op jit(solution)/shard_map/reduce_scatter | solution.py:43
Sparse Core Ops, SparseCore 0:
  9.7 34.7 all-gather.4
  46.6 354.7 all-gather.2
  404.3 31.3 reduce-scatter.1
where the time goes:
time: 445 us; the launch traced here: 442 us
  waiting for transfers between devices  285 us (64%)
  starting transfers between devices  84.1 us (19%)
  matrix products  35.2 us (8%)
  local copies, waits for them, and re-layouts  24.1 us (5%)
  between operations  13.8 us (3%)
    all_to_all x1, waiting for transfers between devices, local(): lax.all_to_all(outgoing, 'qry', split_axis=0, concat_axis=0, tiled=True)  232 us
    all_to_all x1, starting transfers between devices, local(): lax.all_to_all(results, 'qry', split_axis=0, concat_axis=0, tiled=True)  76.1 us
    all_to_all x1, waiting for transfers between devices, local(): lax.all_to_all(results, 'qry', split_axis=0, concat_axis=0, tiled=True)  24.6 us
    dot_general x1, matrix products, local(): jnp.einsum('srf,sqf->srq', own_rows, arrived, precision=lax.Precision.HIG...  20.3 us
    reduce_scatter x1, waiting for transfers between devices, local(): lax.psum_scatter(partial_value, 'ex', scatter_dimension=2, tiled=True)  19.4 us
    dot_general x1, matrix products, local(): lax.dot_general(lax.all_gather(train_proj, 'qry', axis=1, tiled=True), qu...  14.9 us
    gather x1, local copies, waits for them, and re-layouts, local(): own_rows = block_view[pick_block]  11.6 us
    gather x1, local copies, waits for them, and re-layouts, local(): outgoing = tile_view[pick_tile]  10.1 us
  transfers between devices with their start and end apart: 5, of which 4 were waited for; matrix products, arithmetic and copies ran while one was open for 13% of the time, Pallas kernels for 0%

commit v1 on v0

v1 whole, which is shorter than its diff:
```python
import functools

import jax
import jax.numpy as jnp
from jax import lax
from jax.experimental import pallas as pl
from jax.experimental.pallas import tpu as pltpu
from jax.sharding import PartitionSpec as P

BLOCK_ROWS = 128
CANDS = 2
RING = 4
TOP = 32752.0
MESH = pl.DeviceIdType.MESH
MIB = 1 << 20


def code_kernel(pick_ref, rows_ref, codes_ref, scale_ref):
    rows = rows_ref[0]
    top = jnp.maximum(jnp.max(jnp.abs(rows), axis=1, keepdims=True), 1e-30)
    codes_ref[0] = jnp.round(rows * (TOP / top)).astype(jnp.int32).astype(jnp.int16)
    wide = jnp.broadcast_to(top * (1.0 / TOP), (BLOCK_ROWS, BLOCK_ROWS))
    scale_ref[0] = jnp.transpose(wide)[:8]


def code_slots(pick, train_feat):
    slots = pick.shape[0]
    held, width = train_feat.shape[0] // BLOCK_ROWS, train_feat.shape[1]
    blocks = train_feat.reshape(held, BLOCK_ROWS, width)
    return pl.pallas_call(
        code_kernel,
        grid_spec=pltpu.PrefetchScalarGridSpec(
            num_scalar_prefetch=1,
            grid=(slots,),
            in_specs=[pl.BlockSpec((1, BLOCK_ROWS, width), lambda d, pick: (pick[d], 0, 0))],
            out_specs=[
                pl.BlockSpec((1, BLOCK_ROWS, width), lambda d, pick: (d, 0, 0)),
                pl.BlockSpec((1, 8, BLOCK_ROWS), lambda d, pick: (d, 0, 0)),
            ],
        ),
        out_shape=[
            jax.ShapeDtypeStruct((slots, BLOCK_ROWS, width), jnp.int16),
            jax.ShapeDtypeStruct((slots, 8, BLOCK_ROWS), jnp.float32),
        ],
        compiler_params=pltpu.CompilerParams(vmem_limit_bytes=24 * MIB),
        name="code_slots",
    )(pick, blocks)


def main_kernel(
    owner_ref, train_ref, query_ref, tiles_ref, codes_ref, scale_ref,
    prod_ref, exact_ref,
    pieces, queries, slots, slot_scale, split, parts, parts_in,
    own_sem, ring_send, ring_recv, query_send, query_recv, slot_send, slot_recv, part_send, part_recv,
):
    ex, qry = lax.axis_index("ex"), lax.axis_index("qry")
    n_ex, n_qry = queries.shape[0], slots.shape[0]
    y, z = qry // RING, qry % RING
    turn = lambda a, d: (a + d) % RING
    at = {
        "y+": turn(y, 1) * RING + z,
        "y-": turn(y, 3) * RING + z,
        "z+": y * RING + turn(z, 1),
        "z-": y * RING + turn(z, 3),
    }

    own = [
        pltpu.make_async_copy(train_ref, pieces.at[0], own_sem.at[0]),
        pltpu.make_async_copy(query_ref, queries.at[ex], own_sem.at[1]),
        pltpu.make_async_copy(codes_ref.at[qry], slots.at[qry], own_sem.at[2]),
        pltpu.make_async_copy(scale_ref.at[qry], slot_scale.at[qry], own_sem.at[3]),
    ]
    for copy in own:
        copy.start()

    barrier = pltpu.get_barrier_semaphore()
    for d in range(1, n_qry):
        there = turn(y, d // RING) * RING + turn(z, d % RING)
        pl.semaphore_signal(barrier, inc=1, device_id={"qry": there}, device_id_type=MESH)
    for d in range(1, n_ex):
        pl.semaphore_signal(barrier, inc=1, device_id={"ex": (ex + d) % n_ex}, device_id_type=MESH)
    pl.semaphore_wait(barrier, n_qry - 1 + n_ex - 1)

    sent = []
    arriving = {}
    count = [0]

    def move(source, target, way):
        (piece, quarter, many), (new_piece, _, _) = source, target
        k = count[0]
        count[0] += 1
        src = train_ref if piece == 0 else pieces.at[piece]
        copy = pltpu.make_async_remote_copy(
            src_ref=src.at[pl.ds(quarter, many)],
            dst_ref=pieces.at[new_piece, pl.ds(quarter, many)],
            send_sem=ring_send.at[k],
            recv_sem=ring_recv.at[k],
            device_id={"qry": at[way]},
            device_id_type=MESH,
        )
        copy.start()
        sent.append(copy)
        arriving[target] = copy

    def landed(*targets):
        for target in targets:
            arriving[target].wait_recv()

    rel = lambda dy, dz: dy * RING + dz

    move((0, 0, 2), (rel(0, 1), 0, 2), "z+")
    move((0, 0, 2), (rel(0, 3), 0, 2), "z-")
    move((0, 2, 2), (rel(1, 0), 2, 2), "y+")
    move((0, 2, 2), (rel(3, 0), 2, 2), "y-")

    slot_copies = []
    for d in range(1, n_qry):
        there = turn(y, d // RING) * RING + turn(z, d % RING)
        for j, (src, dst) in enumerate(((codes_ref, slots), (scale_ref, slot_scale))):
            copy = pltpu.make_async_remote_copy(
                src_ref=src.at[there],
                dst_ref=dst.at[qry],
                send_sem=slot_send.at[j, d],
                recv_sem=slot_recv.at[j, d],
                device_id={"qry": there},
                device_id_type=MESH,
            )
            copy.start()
            slot_copies.append(copy)

    query_copies = []
    for d in range(1, n_ex):
        copy = pltpu.make_async_remote_copy(
            src_ref=query_ref,
            dst_ref=queries.at[ex],
            send_sem=query_send.at[d],
            recv_sem=query_recv.at[d],
            device_id={"ex": (ex + d) % n_ex},
            device_id_type=MESH,
        )
        copy.start()
        query_copies.append(copy)

    def second(piece_of, quarter, ways):
        move((piece_of(0), quarter, 2), (piece_of(1), quarter, 2), ways[0])
        move((piece_of(0), quarter, 2), (piece_of(3), quarter, 2), ways[1])

    def along_y(dz):
        return lambda dy: rel(dy, dz)

    def along_z(dy):
        return lambda dz: rel(dy, dz)

    second(along_y(0), 0, ("y+", "y-"))
    second(along_z(0), 2, ("z+", "z-"))

    @pl.loop(0, split.shape[1])
    def _(t):
        whole = tiles_ref[t]
        high = whole.astype(jnp.bfloat16)
        split[0, t] = high
        split[1, t] = (whole - high.astype(jnp.float32)).astype(jnp.bfloat16)

    for copy in own:
        copy.wait()
    for copy in query_copies:
        copy.wait_recv()

    def multiply(piece, quarter, first=False):
        dy, dz = piece // RING, piece % RING
        column = turn(y, RING - dy) * RING + turn(z, RING - dz)
        block = queries[column // 2, :, pl.ds(pl.multiple_of((column % 2) * 256, 256), 256)]
        for k in range(quarter, quarter + 2):
            value = lax.dot_general(
                pieces[piece, k], block, (((1,), (1,)), ((), ())), preferred_element_type=jnp.float32
            )
            if first:
                prod_ref[k] = value
            else:
                prod_ref[k] += value

    multiply(0, 0, True)
    multiply(0, 2, True)

    def relay(piece, quarter, new_piece, way):
        move((piece, quarter, 1), (new_piece, quarter, 1), way)

    for d, wz, wy, k in ((1, "z+", "y+", 0), (3, "z-", "y-", 1)):
        landed((rel(0, d), 0, 2))
        relay(rel(0, d), k, rel(0, 2), wz)
        second(along_y(d), 0, ("y+", "y-"))
        landed((rel(d, 0), 2, 2))
        relay(rel(d, 0), 2 + k, rel(2, 0), wy)
        second(along_z(d), 2, ("z+", "z-"))
        multiply(rel(0, d), 0)
        multiply(rel(d, 0), 2)
    for k in range(2):
        landed((rel(0, 2), k, 1))
        landed((rel(2, 0), 2 + k, 1))
    second(along_y(2), 0, ("y+", "y-"))
    second(along_z(2), 2, ("z+", "z-"))
    multiply(rel(0, 2), 0)
    multiply(rel(2, 0), 2)

    def pass_on(c):
        for d, wy, wz, k in ((1, "y+", "z+", 0), (3, "y-", "z-", 1)):
            landed((rel(d, c), 0, 2))
            relay(rel(d, c), k, rel(2, c), wy)
            landed((rel(c, d), 2, 2))
            relay(rel(c, d), 2 + k, rel(c, 2), wz)
            multiply(rel(d, c), 0)
            multiply(rel(c, d), 2)

    def finish(c):
        for k in range(2):
            landed((rel(2, c), k, 1))
            landed((rel(c, 2), 2 + k, 1))
        multiply(rel(2, c), 0)
        multiply(rel(c, 2), 2)

    pass_on(0)
    pass_on(1)
    finish(0)
    pass_on(3)
    finish(1)
    pass_on(2)

    for copy in slot_copies:
        copy.wait_recv()

    pairs = parts.shape[1]
    width = slots.shape[2]
    step = 512

    @pl.loop(0, pairs)
    def _(p):
        slot = owner_ref[p]
        tile = p // CANDS
        total = jnp.zeros((BLOCK_ROWS, BLOCK_ROWS), jnp.float32)
        for c in range(0, width, step):
            rows = slots[slot, :, c : c + step].astype(jnp.float32)
            high = rows.astype(jnp.bfloat16)
            low = (rows - high.astype(jnp.float32)).astype(jnp.bfloat16)
            tile_high, tile_low = split[0, tile, :, c : c + step], split[1, tile, :, c : c + step]
            for a, b in ((high, tile_high), (high, tile_low), (low, tile_high)):
                total += lax.dot_general(a, b, (((1,), (1,)), ((), ())), preferred_element_type=jnp.float32)
        tall = jnp.transpose(jnp.broadcast_to(slot_scale[slot][:1], (BLOCK_ROWS, BLOCK_ROWS)))
        parts[:, p] = (total * tall).reshape(parts.shape[0], parts.shape[2], BLOCK_ROWS)

    part_copies = []
    for d in range(1, n_ex):
        there = (ex + d) % n_ex
        copy = pltpu.make_async_remote_copy(
            src_ref=parts.at[there],
            dst_ref=parts_in.at[d],
            send_sem=part_send.at[d],
            recv_sem=part_recv.at[d],
            device_id={"ex": there},
            device_id_type=MESH,
        )
        copy.start()
        part_copies.append(copy)

    finish(3)
    total = parts[ex]
    for d, copy in enumerate(part_copies, 1):
        copy.wait_recv()
        total += parts_in[d]
    exact_ref[...] = total
    finish(2)

    for copy in sent + slot_copies + query_copies + part_copies:
        copy.wait_send()


def local(train_proj, query_proj, out_weight, train_feat, query_feat, candidates):
    n_qry, n_ex = lax.axis_size("qry"), lax.axis_size("ex")
    my_index = lax.axis_index("qry")
    width = train_feat.shape[1]
    held_blocks = train_feat.shape[0] // BLOCK_ROWS
    tiles_here = query_feat.shape[0] // BLOCK_ROWS
    pairs = tiles_here * CANDS
    items = candidates.reshape(n_qry, pairs)
    wanted_here = items // held_blocks == my_index
    pick = jnp.sum(jnp.where(wanted_here, items % held_blocks, 0), axis=1)
    my_owner = lax.dynamic_slice_in_dim(items, my_index, 1, 0)[0] // held_blocks
    codes, scale = code_slots(pick, train_feat)

    rows, depth = train_proj.shape
    columns, part_depth = query_proj.shape
    share = BLOCK_ROWS // n_ex
    any_space, vmem = pl.BlockSpec(memory_space=pl.ANY), pl.BlockSpec(memory_space=pltpu.VMEM)
    dma = pltpu.SemaphoreType.DMA
    products, exact = pl.pallas_call(
        main_kernel,
        out_shape=[
            jax.ShapeDtypeStruct((4, rows // 4, columns), jnp.float32),
            jax.ShapeDtypeStruct((pairs, share, BLOCK_ROWS), jnp.float32),
        ],
        in_specs=[pl.BlockSpec(memory_space=pltpu.SMEM), any_space, any_space, vmem, any_space, any_space],
        out_specs=[vmem, vmem],
        scratch_shapes=[
            pltpu.VMEM((n_qry, 4, rows // 4, depth), jnp.bfloat16),
            pltpu.VMEM((n_ex, columns, part_depth), jnp.bfloat16),
            pltpu.VMEM((n_qry, BLOCK_ROWS, width), jnp.int16),
            pltpu.VMEM((n_qry, 8, BLOCK_ROWS), jnp.float32),
            pltpu.VMEM((2, tiles_here, BLOCK_ROWS, width), jnp.bfloat16),
            pltpu.VMEM((n_ex, pairs, share, BLOCK_ROWS), jnp.float32),
            pltpu.VMEM((n_ex, pairs, share, BLOCK_ROWS), jnp.float32),
            dma((4,)),
            dma((40,)),
            dma((40,)),
            dma((n_ex,)),
            dma((n_ex,)),
            dma((2, n_qry)),
            dma((2, n_qry)),
            dma((n_ex,)),
            dma((n_ex,)),
        ],
        compiler_params=pltpu.CompilerParams(
            collective_id=0, has_side_effects=True, vmem_limit_bytes=58 * MIB
        ),
        name="main",
    )(
        my_owner,
        train_proj.reshape(4, rows // 4, depth),
        query_proj,
        query_feat.reshape(tiles_here, BLOCK_ROWS, width),
        codes,
        scale,
    )
    scores = products.reshape(rows, columns) * out_weight[:, None]
    return scores, exact.reshape(tiles_here, CANDS, share, BLOCK_ROWS)


def solution(mesh):
    placed = (P("ex", "qry"), P("qry", "ex"), P("ex"), P("qry", "ex"), P("qry", "ex"), P())
    return jax.shard_map(
        local,
        mesh=mesh,
        in_specs=placed,
        out_specs=(P("ex", "qry"), P("qry", None, "ex", None)),
        check_vma=False,
    )
```

time: 445 us -> 265 us (0.60)
  waiting for transfers between devices: 285 us -> 0 us
  Pallas kernels: 0 us -> 249 us
  starting transfers between devices: 84.1 us -> 0 us
  matrix products: 35.2 us -> 0 us
  local copies, waits for them, and re-layouts: 24.1 us -> 8.78 us
  between operations: 13.8 us -> 0.68 us
  other arithmetic: 0.3 us -> 5.92 us
    all_to_all x2 -> x0, waiting for transfers between devices: 256 us -> none  [the longest x1 232 us: local(): lax.all_to_all(outgoing, 'qry', split_axis=0, concat_axis=0, tiled=True)]
    pallas_call x0 -> x2, Pallas kernels: none -> 249 us  [the longest x1 246 us: local(): pl.pallas_call(main_kernel, out_shape=[jax.ShapeDtypeStruct((4, rows // 4...]
    all_to_all x2 -> x0, starting transfers between devices: 84 us -> none  [the longest x1 76.1 us: local(): lax.all_to_all(results, 'qry', split_axis=0, concat_axis=0, tiled=True)]
    dot_general x2 -> x0, matrix products: 35.2 us -> none  [the longest x1 20.3 us: local(): jnp.einsum('srf,sqf->srq', own_rows, arrived, precision=lax.Precision.HIG...]
    gather x3 -> x0, local copies, waits for them, and re-layouts: 23.1 us -> none  [the longest x1 11.6 us: local(): own_rows = block_view[pick_block]]
    reduce_scatter x1 -> x0, waiting for transfers between devices: 19.4 us -> none  [local(): lax.psum_scatter(partial_value, 'ex', scatter_dimension=2, tiled=True)]
    unnamed x5 -> x12, local copies, waits for them, and re-layouts: 0.78 us -> 8.63 us
    all_gather x2 -> x0, waiting for transfers between devices: 7.79 us -> none  [the longest x1 7.77 us: local(): lax.all_gather(train_proj, 'qry', axis=1, tiled=True)]
  transfers between devices with their start and end apart: 5 -> 0, of which waited for: 4 -> 0; matrix products, arithmetic and copies ran while one was open for 13% -> 0% of each run, Pallas kernels for 0% -> 0%
where the time goes in v1:
time: 265 us
  Pallas kernels  249 us (94%)
  local copies, waits for them, and re-layouts  8.78 us (3%)
  other arithmetic  5.92 us (2%)
    pallas_call x1, Pallas kernels, local(): pl.pallas_call(main_kernel, out_shape=[jax.ShapeDtypeStruct((4, rows // 4...  246 us
    unnamed x12, local copies, waits for them, and re-layouts  8.63 us

profile of v1, /device:TPU:9, one launch (start us, length us, event | category | flops | bytes accessed | tf_op | source)
XLA Modules:
  0.0 264.7 jit_solution(13527983456194117817)
XLA Ops:
  0.6 0.7 fusion
  1.3 0.1 reduce_sum.14
  1.4 0.1 reduce_sum.18.pick_ref
  1.5 0.8 copy.9
  2.3 0.1 reshape.24
  2.4 0.5 and_select_fusion.2.owner_ref
  2.9 0.0 copy-start
  2.9 3.4 %copy-done = f32[1024,2048]{1,0:T(8,128)S(1)} copy-done((f32[1024,2048]{1,0:T(8,128)S(1)}, f32[1024,2048]{1,0:T(8,128)}, u32[]{:S(2)}) %copy-start) | copy-done | bytes 8388632
  6.3 3.8 %code_slots.1 = (s16[16,128,2048]{2,1,0:T(8,128)(2,1)S(1)}, f32[16,8,128]{2,1,0:T(8,128)S(1)}) custom-call(s32[16]{0:T(128)S(1)} %reduce_sum.18.pick_ref, f32[8,128,2048]{2,1,0:T(8,128)S(1)} %bitcast.14), custom_call_target="tpu_custom_call" | custom-call | tf_op jit(solution)/shard_map/code_slots/pallas_call | solution.py:30
  10.1 0.0 copy-start.1
  10.1 3.2 %copy-done.1 = s16[16,128,2048]{2,1,0:T(8,128)(2,1)} copy-done((s16[16,128,2048]{2,1,0:T(8,128)(2,1)}, s16[16,128,2048]{2,1,0:T(8,128)(2,1)S(1)}, u32[]{:S(2)}) %copy-start.1) | copy-done | bytes 8388632
  13.3 0.0 copy-start.2
  13.3 0.6 copy-done.2
  13.9 0.0 copy-start.4
  13.9 245.6 %main.1 = (f32[4,512,512]{2,1,0:T(8,128)}, f32[8,16,128]{2,1,0:T(8,128)}) custom-call(s32[8]{0:T(128)} %and_select_fusion.2.owner_ref, bf16[4,512,256]{2,1,0:T(8,128)(2,1)} %bitcast.16, bf16[512,512]{1,0:T(8,128)(2,1)} %query_ref.1, f32[4,128,2048]{2,1,0:T(8,128)} %bitcast.15, s16[16,128,2048]{2,1,0:T(8,128)(2,1)} %copy-done.1, f32[16,8,128]{2,1,0:T(8,128)} %copy-done.2), custom_call_target="tpu_custom_call" | custom-call | tf_op jit(solution)/shard_map/main/pallas_call | solution.py:294
  259.5 0.0 copy-done.4
  259.5 0.0 copy-start.3
  259.5 4.6 %bitcast_multiply_fusion = f32[2048,512]{1,0:T(8,128)} fusion(f32[4,512,512]{2,1,0:T(8,128)} %get-tuple-element.8, f32[2048]{0:T(1024)S(1)} %copy-done.4), kind=kLoop, calls=%fused_computation | loop fusion | flops 1048576 | bytes 8396800 | tf_op jit(solution)/shard_map/mul | solution.py:332
  264.1 0.0 copy-done.3
  264.1 0.6 copy.11
Async XLA Ops:
  2.9 3.4 %copy-start = (f32[1024,2048]{1,0:T(8,128)S(1)}, f32[1024,2048]{1,0:T(8,128)}, u32[]{:S(2)}) copy-start(f32[1024,2048]{1,0:T(8,128)} %param.9) | copy-start | bytes 25165828
  10.1 3.2 %copy-start.1 = (s16[16,128,2048]{2,1,0:T(8,128)(2,1)}, s16[16,128,2048]{2,1,0:T(8,128)(2,1)S(1)}, u32[]{:S(2)}) copy-start(s16[16,128,2048]{2,1,0:T(8,128)(2,1)S(1)} %get-tuple-element.6.codes_ref) | copy-start | bytes 25165828
  13.3 0.6 copy-start.2
  13.9 245.6 %copy-start.4 = (f32[2048]{0:T(1024)S(1)}, f32[2048]{0:T(1024)}, u32[]{:S(2)}) copy-start(f32[2048]{0:T(1024)} %param.8) | copy-start | bytes 24580
  259.5 4.6 %copy-start.3 = (f32[8,16,128]{2,1,0:T(8,128)S(1)}, f32[8,16,128]{2,1,0:T(8,128)}, u32[]{:S(2)}) copy-start(f32[8,16,128]{2,1,0:T(8,128)} %get-tuple-element.9) | copy-start | bytes 196612

commit v2 on v0

v2 whole, which is shorter than its diff:
```python
import functools

import jax
import jax.numpy as jnp
from jax import lax
from jax.experimental import pallas as pl
from jax.experimental.pallas import tpu as pltpu
from jax.sharding import PartitionSpec as P

BLOCK_ROWS = 128
CANDS = 2
RING = 4
SLOT_CHUNKS = 4
COPIES = 144
TOP = 32752.0
MESH = pl.DeviceIdType.MESH
MIB = 1 << 20


def code_kernel(pick_ref, rows_ref, codes_ref, scale_ref):
    rows = rows_ref[0]
    top = jnp.maximum(jnp.max(jnp.abs(rows), axis=1, keepdims=True), 1e-30)
    codes_ref[0] = jnp.round(rows * (TOP / top)).astype(jnp.int32).astype(jnp.int16)
    wide = jnp.broadcast_to(top * (1.0 / TOP), (BLOCK_ROWS, BLOCK_ROWS))
    scale_ref[0] = jnp.transpose(wide)[:8]


def code_slots(pick, train_feat):
    slots = pick.shape[0]
    held, width = train_feat.shape[0] // BLOCK_ROWS, train_feat.shape[1]
    blocks = train_feat.reshape(held, BLOCK_ROWS, width)
    return pl.pallas_call(
        code_kernel,
        grid_spec=pltpu.PrefetchScalarGridSpec(
            num_scalar_prefetch=1,
            grid=(slots,),
            in_specs=[pl.BlockSpec((1, BLOCK_ROWS, width), lambda d, pick: (pick[d], 0, 0))],
            out_specs=[
                pl.BlockSpec((1, BLOCK_ROWS, width), lambda d, pick: (d, 0, 0)),
                pl.BlockSpec((1, 8, BLOCK_ROWS), lambda d, pick: (d, 0, 0)),
            ],
        ),
        out_shape=[
            jax.ShapeDtypeStruct((slots, BLOCK_ROWS, width), jnp.int16),
            jax.ShapeDtypeStruct((slots, 8, BLOCK_ROWS), jnp.float32),
        ],
        compiler_params=pltpu.CompilerParams(vmem_limit_bytes=24 * MIB),
        name="code_slots",
    )(pick, blocks)


def main_kernel(
    owner_ref, train_ref, query_ref, tiles_ref, codes_ref, scale_ref,
    out_ref, out_scale_ref, exact_ref,
    trains, queries, slots, slot_scale, tiles, split, products, ready, ready_scale, parts, parts_in,
    own_sem, send_sem, recv_sem,
):
    ex, qry = lax.axis_index("ex"), lax.axis_index("qry")
    n_ex, n_qry = parts.shape[0], slots.shape[0]
    x, core, y, z = ex // 2, ex % 2, qry // RING, qry % RING
    turn = lambda a, d: (a + d) % RING
    sent = []

    def send(src, dst, dx=0, dc=0, dy=0, dz=0):
        there = {"ex": turn(x, dx) * 2 + (core + dc) % 2, "qry": turn(y, dy) * RING + turn(z, dz)}
        k = len(sent)
        copy = pltpu.make_async_remote_copy(
            src_ref=src,
            dst_ref=dst,
            send_sem=send_sem.at[k],
            recv_sem=recv_sem.at[k],
            device_id=there,
            device_id_type=MESH,
        )
        copy.start()
        sent.append(copy)
        return copy

    rows, width = trains.shape[1], slots.shape[2]
    depth, part_depth = train_ref.shape[2], query_ref.shape[1]
    half = rows // 2
    my_depth = pl.ds(pl.multiple_of(z * depth, depth), depth)
    my_part = pl.ds(pl.multiple_of(core * part_depth, part_depth), part_depth)

    own = [
        pltpu.make_async_copy(train_ref.at[z], trains.at[y, :, my_depth], own_sem.at[0]),
        pltpu.make_async_copy(query_ref, queries.at[x, z, :, my_part], own_sem.at[1]),
        pltpu.make_async_copy(codes_ref.at[qry], slots.at[qry], own_sem.at[2]),
        pltpu.make_async_copy(scale_ref.at[qry], slot_scale.at[qry], own_sem.at[3]),
        pltpu.make_async_copy(tiles_ref, tiles, own_sem.at[4]),
    ]
    for copy in own:
        copy.start()

    barrier = pltpu.get_barrier_semaphore()
    for d in range(1, n_qry):
        there = turn(y, d // RING) * RING + turn(z, d % RING)
        pl.semaphore_signal(barrier, inc=1, device_id={"qry": there}, device_id_type=MESH)
    for d in range(1, n_ex):
        there = turn(x, d // 2) * 2 + (core + d % 2) % 2
        pl.semaphore_signal(barrier, inc=1, device_id={"ex": there}, device_id_type=MESH)
    pl.semaphore_wait(barrier, n_qry - 1 + n_ex - 1)

    def query_half(at_x, at_z, h):
        return queries.at[at_x, at_z, pl.ds(h * half, half), my_part]

    def query_sends(source, at_z):
        out = {}
        for h in range(2):
            for d in (1, 3):
                out[d, h] = send(source(h), query_half(x, at_z, h), dx=d)
        return out

    near_z = {}
    for h in range(2):
        for d in (1, 3):
            near_z[d, h] = send(query_ref.at[pl.ds(h * half, half)], query_half(x, z, h), dz=d)
    along_x = {0: query_sends(lambda h: query_ref.at[pl.ds(h * half, half)], z)}
    train_z = [
        send(train_ref.at[turn(z, d)], trains.at[y, :, my_depth], dz=d) for d in (1, 3, 2)
    ]

    slot_copies = []
    order = ((0, 1), (1, 0), (0, 3), (3, 0), (1, 1), (3, 3), (1, 3), (3, 1), (2, 1), (1, 2), (2, 3), (3, 2), (0, 2), (2, 0), (2, 2))
    chunk = BLOCK_ROWS // SLOT_CHUNKS

    def slot_round(r):
        for dy, dz in order:
            there = turn(y, dy) * RING + turn(z, dz)
            if r == 0:
                slot_copies.append(send(scale_ref.at[there], slot_scale.at[qry], dy=dy, dz=dz))
            part = pl.ds(r * chunk, chunk)
            slot_copies.append(send(codes_ref.at[there, part], slots.at[qry, part], dy=dy, dz=dz))

    slot_round(0)

    near_z[1, 0].wait_recv()
    far_z = {0: send(query_half(x, turn(z, 3), 0), query_half(x, turn(z, 3), 0), dz=1)}
    near_z[3, 1].wait_recv()
    far_z[1] = send(query_half(x, turn(z, 1), 1), query_half(x, turn(z, 1), 1), dz=3)
    near_z[1, 1].wait_recv()
    along_x[3] = query_sends(lambda h: query_half(x, turn(z, 3), h), turn(z, 3))
    near_z[3, 0].wait_recv()
    along_x[1] = query_sends(lambda h: query_half(x, turn(z, 1), h), turn(z, 1))

    for copy in train_z:
        copy.wait_recv()
    own[0].wait()

    def train_half(at_y, h):
        return trains.at[at_y, pl.ds(h * half, half)]

    near_y = {}
    for h in range(2):
        for d in (1, 3):
            near_y[d, h] = send(train_half(y, h), train_half(y, h), dy=d)
    slot_round(1)

    def relay_x(d):
        at_z = turn(z, d)
        along_x[d][1, 0].wait_recv()
        first = send(query_half(turn(x, 3), at_z, 0), query_half(turn(x, 3), at_z, 0), dx=1)
        along_x[d][3, 1].wait_recv()
        second = send(query_half(turn(x, 1), at_z, 1), query_half(turn(x, 1), at_z, 1), dx=3)
        return first, second

    far_x = {0: relay_x(0)}

    far_z[0].wait_recv()
    far_z[1].wait_recv()
    along_x[2] = query_sends(lambda h: query_half(x, turn(z, 2), h), turn(z, 2))
    own[1].wait()

    def to_core(at_x):
        view = queries.at[at_x, :, :, my_part]
        return send(view, view, dc=1)

    from_core = {0: to_core(x)}

    near_y[1, 0].wait_recv()
    far_y = {0: send(train_half(turn(y, 3), 0), train_half(turn(y, 3), 0), dy=1)}
    near_y[3, 1].wait_recv()
    far_y[1] = send(train_half(turn(y, 1), 1), train_half(turn(y, 1), 1), dy=3)
    slot_round(2)

    own[4].wait()

    @pl.loop(0, split.shape[1])
    def _(t):
        whole = tiles[t]
        high = whole.astype(jnp.bfloat16)
        split[0, t] = high
        split[1, t] = (whole - high.astype(jnp.float32)).astype(jnp.bfloat16)

    far_x[3] = relay_x(3)
    far_x[1] = relay_x(1)
    slot_round(3)
    near_y[1, 1].wait_recv()
    near_y[3, 0].wait_recv()
    far_y[0].wait_recv()
    far_y[1].wait_recv()

    def multiply(at_x, first=False):
        from_core[at_x].wait_recv()
        place = turn(x, at_x)

        @pl.loop(0, RING)
        def _(to):
            value = lax.dot_general(
                trains[place], queries[place, to], (((1,), (1,)), ((), ())), preferred_element_type=jnp.float32
            )
            if first:
                products[to] = value
            else:
                products[to] += value

    multiply(0, True)
    far_x[2] = relay_x(2)
    for d in range(RING):
        along_x[d][1, 1].wait_recv()
        along_x[d][3, 0].wait_recv()
    from_core[3] = to_core(turn(x, 3))
    from_core[1] = to_core(turn(x, 1))
    multiply(3)
    multiply(1)
    for d in range(RING):
        far_x[d][0].wait_recv()
        far_x[d][1].wait_recv()
    from_core[2] = to_core(turn(x, 2))
    multiply(2)

    @pl.loop(0, RING)
    def _(to):
        value = products[to]
        top = jnp.maximum(jnp.max(jnp.abs(value), axis=1, keepdims=True), 1e-30)
        ready[to] = jnp.round(value * (TOP / top)).astype(jnp.int32).astype(jnp.int16)
        ready_scale[to] = jnp.transpose(jnp.broadcast_to(top * (1.0 / TOP), (rows, 128)))[:8]

    out_copies = []
    for d in (1, 3, 2):
        out_copies.append(send(ready_scale.at[turn(z, d)], out_scale_ref.at[z], dz=d))
        for h in range(2):
            part = pl.ds(h * half, half)
            out_copies.append(send(ready.at[turn(z, d), part], out_ref.at[z, part], dz=d))
    stay = [
        pltpu.make_async_copy(ready.at[z], out_ref.at[z], own_sem.at[5]),
        pltpu.make_async_copy(ready_scale.at[z], out_scale_ref.at[z], own_sem.at[6]),
    ]
    for copy in stay:
        copy.start()

    own[2].wait()
    own[3].wait()
    for copy in slot_copies:
        copy.wait_recv()
    step = 512

    @pl.loop(0, parts.shape[1])
    def _(p):
        slot = owner_ref[p]
        tile = p // CANDS
        total = jnp.zeros((BLOCK_ROWS, BLOCK_ROWS), jnp.float32)
        for c in range(0, width, step):
            block = slots[slot, :, c : c + step].astype(jnp.float32)
            high = block.astype(jnp.bfloat16)
            low = (block - high.astype(jnp.float32)).astype(jnp.bfloat16)
            tile_high, tile_low = split[0, tile, :, c : c + step], split[1, tile, :, c : c + step]
            for a, b in ((high, tile_high), (high, tile_low), (low, tile_high)):
                total += lax.dot_general(a, b, (((1,), (1,)), ((), ())), preferred_element_type=jnp.float32)
        tall = jnp.transpose(jnp.broadcast_to(slot_scale[slot][:1], (BLOCK_ROWS, BLOCK_ROWS)))
        parts[:, p] = (total * tall).reshape(parts.shape[0], parts.shape[2], BLOCK_ROWS)

    part_copies = []
    for d in range(1, n_ex):
        there = turn(x, d // 2) * 2 + (core + d % 2) % 2
        part_copies.append(send(parts.at[there], parts_in.at[d], dx=d // 2, dc=d % 2))
    total = parts[ex]
    for d, copy in enumerate(part_copies, 1):
        copy.wait_recv()
        total += parts_in[d]
    exact_ref[...] = total

    for copy in out_copies:
        copy.wait_recv()
    for copy in stay:
        copy.wait()
    for copy in sent:
        copy.wait_send()


def decode_kernel(codes_ref, scale_ref, weight_ref, scores_ref):
    line = scale_ref[0][:1] * weight_ref[0]
    tall = jnp.transpose(jnp.broadcast_to(line, (128, line.shape[1])))
    scores_ref[...] = codes_ref[0].astype(jnp.float32) * tall[:, :1]


def local(train_proj, query_proj, out_weight, train_feat, query_feat, candidates):
    n_qry, n_ex = lax.axis_size("qry"), lax.axis_size("ex")
    my_index = lax.axis_index("qry")
    width = train_feat.shape[1]
    held_blocks = train_feat.shape[0] // BLOCK_ROWS
    tiles_here = query_feat.shape[0] // BLOCK_ROWS
    pairs = tiles_here * CANDS
    items = candidates.reshape(n_qry, pairs)
    wanted_here = items // held_blocks == my_index
    pick = jnp.sum(jnp.where(wanted_here, items % held_blocks, 0), axis=1)
    my_owner = lax.dynamic_slice_in_dim(items, my_index, 1, 0)[0] // held_blocks
    codes, scale = code_slots(pick, train_feat)

    depth = train_proj.shape[1]
    rows = train_proj.shape[0] // RING
    columns, part_depth = query_proj.shape
    share = BLOCK_ROWS // n_ex
    any_space, vmem = pl.BlockSpec(memory_space=pl.ANY), pl.BlockSpec(memory_space=pltpu.VMEM)
    dma = pltpu.SemaphoreType.DMA
    result, result_scale, exact = pl.pallas_call(
        main_kernel,
        out_shape=[
            jax.ShapeDtypeStruct((RING, rows, columns), jnp.int16),
            jax.ShapeDtypeStruct((RING, 8, rows), jnp.float32),
            jax.ShapeDtypeStruct((pairs, share, BLOCK_ROWS), jnp.float32),
        ],
        in_specs=[pl.BlockSpec(memory_space=pltpu.SMEM)] + [any_space] * 5,
        out_specs=[vmem, vmem, vmem],
        scratch_shapes=[
            pltpu.VMEM((RING, rows, RING * depth), jnp.bfloat16),
            pltpu.VMEM((RING, RING, columns, 2 * part_depth), jnp.bfloat16),
            pltpu.VMEM((n_qry, BLOCK_ROWS, width), jnp.int16),
            pltpu.VMEM((n_qry, 8, BLOCK_ROWS), jnp.float32),
            pltpu.VMEM((tiles_here, BLOCK_ROWS, width), jnp.float32),
            pltpu.VMEM((2, tiles_here, BLOCK_ROWS, width), jnp.bfloat16),
            pltpu.VMEM((RING, rows, columns), jnp.float32),
            pltpu.VMEM((RING, rows, columns), jnp.int16),
            pltpu.VMEM((RING, 8, rows), jnp.float32),
            pltpu.VMEM((n_ex, pairs, share, BLOCK_ROWS), jnp.float32),
            pltpu.VMEM((n_ex, pairs, share, BLOCK_ROWS), jnp.float32),
            dma((8,)),
            dma((COPIES,)),
            dma((COPIES,)),
        ],
        compiler_params=pltpu.CompilerParams(
            collective_id=0, has_side_effects=True, vmem_limit_bytes=58 * MIB
        ),
        name="main",
    )(
        my_owner,
        train_proj.reshape(RING, rows, depth),
        query_proj,
        query_feat.reshape(tiles_here, BLOCK_ROWS, width),
        codes,
        scale,
    )
    scores = pl.pallas_call(
        decode_kernel,
        grid=(RING,),
        in_specs=[
            pl.BlockSpec((1, rows, columns), lambda i: (i, 0, 0)),
            pl.BlockSpec((1, 8, rows), lambda i: (i, 0, 0)),
            pl.BlockSpec((1, 1, rows), lambda i: (i, 0, 0)),
        ],
        out_specs=pl.BlockSpec((rows, columns), lambda i: (i, 0)),
        out_shape=jax.ShapeDtypeStruct((RING * rows, columns), jnp.float32),
        compiler_params=pltpu.CompilerParams(vmem_limit_bytes=24 * MIB),
        name="decode",
    )(result, result_scale, out_weight.reshape(RING, 1, rows))
    return scores, exact.reshape(tiles_here, CANDS, share, BLOCK_ROWS)


def solution(mesh):
    placed = (P("ex", "qry"), P("qry", "ex"), P("ex"), P("qry", "ex"), P("qry", "ex"), P())
    return jax.shard_map(
        local,
        mesh=mesh,
        in_specs=placed,
        out_specs=(P("ex", "qry"), P("qry", None, "ex", None)),
        check_vma=False,
    )
```

time: 445 us -> 197 us (0.44)
  waiting for transfers between devices: 285 us -> 0 us
  Pallas kernels: 0 us -> 184 us
  starting transfers between devices: 84.1 us -> 0 us
  matrix products: 35.2 us -> 0 us
  between operations: 13.8 us -> 0.68 us
  local copies, waits for them, and re-layouts: 24.1 us -> 11.2 us
    all_to_all x2 -> x0, waiting for transfers between devices: 256 us -> none  [the longest x1 232 us: local(): lax.all_to_all(outgoing, 'qry', split_axis=0, concat_axis=0, tiled=True)]
    pallas_call x0 -> x3, Pallas kernels: none -> 184 us  [the longest x1 177 us: local(): pl.pallas_call(main_kernel, out_shape=[jax.ShapeDtypeStruct((RING, rows,...]
    all_to_all x2 -> x0, starting transfers between devices: 84 us -> none  [the longest x1 76.1 us: local(): lax.all_to_all(results, 'qry', split_axis=0, concat_axis=0, tiled=True)]
    dot_general x2 -> x0, matrix products: 35.2 us -> none  [the longest x1 20.3 us: local(): jnp.einsum('srf,sqf->srq', own_rows, arrived, precision=lax.Precision.HIG...]
    gather x3 -> x0, local copies, waits for them, and re-layouts: 23.1 us -> none  [the longest x1 11.6 us: local(): own_rows = block_view[pick_block]]
    reduce_scatter x1 -> x0, waiting for transfers between devices: 19.4 us -> none  [local(): lax.psum_scatter(partial_value, 'ex', scatter_dimension=2, tiled=True)]
    unnamed x5 -> x16, local copies, waits for them, and re-layouts: 0.78 us -> 11.1 us
    all_gather x2 -> x0, waiting for transfers between devices: 7.79 us -> none  [the longest x1 7.77 us: local(): lax.all_gather(train_proj, 'qry', axis=1, tiled=True)]
  transfers between devices with their start and end apart: 5 -> 0, of which waited for: 4 -> 0; matrix products, arithmetic and copies ran while one was open for 13% -> 0% of each run, Pallas kernels for 0% -> 0%
where the time goes in v2:
time: 197 us
  Pallas kernels  184 us (93%)
  local copies, waits for them, and re-layouts  11.2 us (6%)
    pallas_call x1, Pallas kernels, local(): pl.pallas_call(main_kernel, out_shape=[jax.ShapeDtypeStruct((RING, rows,...  177 us
    unnamed x16, local copies, waits for them, and re-layouts  11.1 us

profile of v2, /device:TPU:9, one launch (start us, length us, event | category | flops | bytes accessed | tf_op | source)
XLA Modules:
  0.0 196.9 jit_solution(12700184447572937282)
XLA Ops:
  0.6 0.7 fusion
  1.3 0.1 reduce_sum.14
  1.4 0.1 reduce_sum.18.pick_ref
  1.5 0.8 copy.9
  2.3 0.1 reshape.23
  2.4 0.5 and_select_fusion.2.owner_ref
  2.9 0.0 copy-start
  2.9 3.4 %copy-done = f32[1024,2048]{1,0:T(8,128)S(1)} copy-done((f32[1024,2048]{1,0:T(8,128)S(1)}, f32[1024,2048]{1,0:T(8,128)}, u32[]{:S(2)}) %copy-start) | copy-done | bytes 8388632
  6.3 3.8 %code_slots.1 = (s16[16,128,2048]{2,1,0:T(8,128)(2,1)S(1)}, f32[16,8,128]{2,1,0:T(8,128)S(1)}) custom-call(s32[16]{0:T(128)S(1)} %reduce_sum.18.pick_ref, f32[8,128,2048]{2,1,0:T(8,128)S(1)} %bitcast.13), custom_call_target="tpu_custom_call" | custom-call | tf_op jit(solution)/shard_map/code_slots/pallas_call | solution.py:32
  10.1 0.0 copy-start.1
  10.1 3.2 %copy-done.1 = s16[16,128,2048]{2,1,0:T(8,128)(2,1)} copy-done((s16[16,128,2048]{2,1,0:T(8,128)(2,1)}, s16[16,128,2048]{2,1,0:T(8,128)(2,1)S(1)}, u32[]{:S(2)}) %copy-start.1) | copy-done | bytes 8388632
  13.3 0.0 copy-start.3
  13.3 0.6 copy-done.3
  13.9 0.0 copy-start.5
  13.9 177.1 %main.1 = (s16[4,512,512]{2,1,0:T(8,128)(2,1)}, f32[4,8,512]{2,1,0:T(8,128)}, f32[8,16,128]{2,1,0:T(8,128)}) custom-call(s32[8]{0:T(128)} %and_select_fusion.2.owner_ref, bf16[4,512,256]{2,1,0:T(8,128)(2,1)} %bitcast.16, bf16[512,512]{1,0:T(8,128)(2,1)} %query_ref.1, f32[4,128,2048]{2,1,0:T(8,128)} %bitcast.15, s16[16,128,2048]{2,1,0:T(8,128)(2,1)} %copy-done.1, ...), custom_call_target="tpu_custom_call" | custom-call | tf_op jit(solution)/shard_map/main/pallas_call | solution.py:316
  191.0 0.0 copy-done.5
  191.0 0.0 copy-start.2
  191.1 1.6 copy-done.2
  192.6 0.0 copy-start.4
  192.6 0.8 copy-done.4
  193.5 0.0 copy-start.6
  193.5 2.7 %decode.1 = f32[2048,512]{1,0:T(8,128)} custom-call(s16[4,512,512]{2,1,0:T(8,128)(2,1)S(1)} %copy-done.2, f32[4,8,512]{2,1,0:T(8,128)S(1)} %copy-done.4, f32[4,1,512]{2,1,0:T(1,128)S(1)} %bitcast.14), custom_call_target="tpu_custom_call" | custom-call | tf_op jit(solution)/shard_map/decode/pallas_call | solution.py:353
  196.2 0.0 copy-done.6
  196.2 0.6 copy.11
Async XLA Ops:
  2.9 3.4 %copy-start = (f32[1024,2048]{1,0:T(8,128)S(1)}, f32[1024,2048]{1,0:T(8,128)}, u32[]{:S(2)}) copy-start(f32[1024,2048]{1,0:T(8,128)} %param.9) | copy-start | bytes 25165828
  10.1 3.2 %copy-start.1 = (s16[16,128,2048]{2,1,0:T(8,128)(2,1)}, s16[16,128,2048]{2,1,0:T(8,128)(2,1)S(1)}, u32[]{:S(2)}) copy-start(s16[16,128,2048]{2,1,0:T(8,128)(2,1)S(1)} %get-tuple-element.7.codes_ref) | copy-start | bytes 25165828
  13.3 0.6 copy-start.3
  13.9 177.1 %copy-start.5 = (f32[2048]{0:T(1024)S(1)}, f32[2048]{0:T(1024)}, u32[]{:S(2)}) copy-start(f32[2048]{0:T(1024)} %param.8) | copy-start | bytes 24580
  191.0 1.6 copy-start.2
  192.6 0.8 copy-start.4
  193.5 2.8 %copy-start.6 = (f32[8,16,128]{2,1,0:T(8,128)S(1)}, f32[8,16,128]{2,1,0:T(8,128)}, u32[]{:S(2)}) copy-start(f32[8,16,128]{2,1,0:T(8,128)} %get-tuple-element.11) | copy-start | bytes 196612

commit v3 on v2

--- a/solution.py
+++ b/solution.py
@@ -1,5 +1,3 @@
-import functools
-
 import jax
 import jax.numpy as jnp
 from jax import lax
@@ -17,43 +15,12 @@
 MIB = 1 << 20
 
 
-def code_kernel(pick_ref, rows_ref, codes_ref, scale_ref):
-    rows = rows_ref[0]
-    top = jnp.maximum(jnp.max(jnp.abs(rows), axis=1, keepdims=True), 1e-30)
-    codes_ref[0] = jnp.round(rows * (TOP / top)).astype(jnp.int32).astype(jnp.int16)
-    wide = jnp.broadcast_to(top * (1.0 / TOP), (BLOCK_ROWS, BLOCK_ROWS))
-    scale_ref[0] = jnp.transpose(wide)[:8]
-
-
-def code_slots(pick, train_feat):
-    slots = pick.shape[0]
-    held, width = train_feat.shape[0] // BLOCK_ROWS, train_feat.shape[1]
-    blocks = train_feat.reshape(held, BLOCK_ROWS, width)
-    return pl.pallas_call(
-        code_kernel,
-        grid_spec=pltpu.PrefetchScalarGridSpec(
-            num_scalar_prefetch=1,
-            grid=(slots,),
-            in_specs=[pl.BlockSpec((1, BLOCK_ROWS, width), lambda d, pick: (pick[d], 0, 0))],
-            out_specs=[
-                pl.BlockSpec((1, BLOCK_ROWS, width), lambda d, pick: (d, 0, 0)),
-                pl.BlockSpec((1, 8, BLOCK_ROWS), lambda d, pick: (d, 0, 0)),
-            ],
-        ),
-        out_shape=[
-            jax.ShapeDtypeStruct((slots, BLOCK_ROWS, width), jnp.int16),
-            jax.ShapeDtypeStruct((slots, 8, BLOCK_ROWS), jnp.float32),
-        ],
-        compiler_params=pltpu.CompilerParams(vmem_limit_bytes=24 * MIB),
-        name="code_slots",
-    )(pick, blocks)
-
-
 def main_kernel(
-    owner_ref, train_ref, query_ref, tiles_ref, codes_ref, scale_ref,
+    cand_ref, train_ref, query_ref, blocks_ref, tiles_ref,
     out_ref, out_scale_ref, exact_ref,
-    trains, queries, slots, slot_scale, tiles, split, products, ready, ready_scale, parts, parts_in,
-    own_sem, send_sem, recv_sem,
+    pick, stage, coded, coded_scale, leaving, leaving_scale,
+    trains, queries, slots, slot_scale, split, product, ready, ready_scale, parts, parts_in,
+    stage_sem, own_sem, send_sem, recv_sem,
 ):
     ex, qry = lax.axis_index("ex"), lax.axis_index("qry")
     n_ex, n_qry = parts.shape[0], slots.shape[0]
@@ -85,12 +52,16 @@
     own = [
         pltpu.make_async_copy(train_ref.at[z], trains.at[y, :, my_depth], own_sem.at[0]),
         pltpu.make_async_copy(query_ref, queries.at[x, z, :, my_part], own_sem.at[1]),
-        pltpu.make_async_copy(codes_ref.at[qry], slots.at[qry], own_sem.at[2]),
-        pltpu.make_async_copy(scale_ref.at[qry], slot_scale.at[qry], own_sem.at[3]),
-        pltpu.make_async_copy(tiles_ref, tiles, own_sem.at[4]),
     ]
     for copy in own:
         copy.start()
+    depth_of_stage = stage.shape[0]
+
+    def fetch(source, index, place):
+        return pltpu.make_async_copy(source.at[index], stage.at[place], stage_sem.at[place])
+
+    for b in range(depth_of_stage):
+        fetch(blocks_ref, b, b).start()
 
     barrier = pltpu.get_barrier_semaphore()
     for d in range(1, n_qry):
@@ -120,6 +91,47 @@
         send(train_ref.at[turn(z, d)], trains.at[y, :, my_depth], dz=d) for d in (1, 3, 2)
     ]
 
+    held = coded.shape[0]
+    pairs = parts.shape[1]
+
+    def wanted(q, p):
+        return cand_ref[q * (pairs // CANDS) + p // CANDS, p % CANDS]
+
+    @pl.loop(0, n_qry)
+    def _(q):
+        block = jnp.int32(0)
+        for p in range(pairs):
+            item = wanted(q, p)
+            block += jnp.where(item // held == qry, item % held, 0)
+        pick[q] = block
+
+    def code(b):
+        place = b % depth_of_stage
+        fetch(blocks_ref, b, place).wait()
+        whole = stage[place]
+        top = jnp.maximum(jnp.max(jnp.abs(whole), axis=1, keepdims=True), 1e-30)
+        coded[b] = jnp.round(whole * (TOP / top)).astype(jnp.int32).astype(jnp.int16)
+        wide = jnp.broadcast_to(top * (1.0 / TOP), (BLOCK_ROWS, BLOCK_ROWS))
+        coded_scale[b] = jnp.transpose(wide)[:8]
+
+    @pl.loop(0, depth_of_stage)
+    def _(b):
+        code(b)
+        fetch(blocks_ref, b + depth_of_stage, b).start()
+
+    @pl.loop(depth_of_stage, held)
+    def _(b):
+        code(b)
+        fetch(tiles_ref, b - depth_of_stage, b - depth_of_stage).start()
+
+    @pl.loop(0, n_qry)
+    def _(q):
+        leaving[q] = coded[pick[q]]
+        leaving_scale[q] = coded_scale[pick[q]]
+
+    slots[qry] = coded[pick[qry]]
+    slot_scale[qry] = coded_scale[pick[qry]]
+
     slot_copies = []
     order = ((0, 1), (1, 0), (0, 3), (3, 0), (1, 1), (3, 3), (1, 3), (3, 1), (2, 1), (1, 2), (2, 3), (3, 2), (0, 2), (2, 0), (2, 2))
     chunk = BLOCK_ROWS // SLOT_CHUNKS
@@ -128,9 +140,9 @@
         for dy, dz in order:
             there = turn(y, dy) * RING + turn(z, dz)
             if r == 0:
-                slot_copies.append(send(scale_ref.at[there], slot_scale.at[qry], dy=dy, dz=dz))
+                slot_copies.append(send(leaving_scale.at[there], slot_scale.at[qry], dy=dy, dz=dz))
             part = pl.ds(r * chunk, chunk)
-            slot_copies.append(send(codes_ref.at[there, part], slots.at[qry, part], dy=dy, dz=dz))
+            slot_copies.append(send(leaving.at[there, part], slots.at[qry, part], dy=dy, dz=dz))
 
     slot_round(0)
 
@@ -169,95 +181,89 @@
     far_z[0].wait_recv()
     far_z[1].wait_recv()
     along_x[2] = query_sends(lambda h: query_half(x, turn(z, 2), h), turn(z, 2))
-    own[1].wait()
-
-    def to_core(at_x):
-        view = queries.at[at_x, :, :, my_part]
-        return send(view, view, dc=1)
-
-    from_core = {0: to_core(x)}
-
     near_y[1, 0].wait_recv()
     far_y = {0: send(train_half(turn(y, 3), 0), train_half(turn(y, 3), 0), dy=1)}
     near_y[3, 1].wait_recv()
     far_y[1] = send(train_half(turn(y, 1), 1), train_half(turn(y, 1), 1), dy=3)
     slot_round(2)
 
-    own[4].wait()
-
     @pl.loop(0, split.shape[1])
     def _(t):
-        whole = tiles[t]
+        fetch(tiles_ref, t, t).wait()
+        whole = stage[t]
         high = whole.astype(jnp.bfloat16)
         split[0, t] = high
         split[1, t] = (whole - high.astype(jnp.float32)).astype(jnp.bfloat16)
 
+    own[1].wait()
+
+    def complete(d):
+        along_x[d][1, 1].wait_recv()
+        along_x[d][3, 0].wait_recv()
+        far_x[d][0].wait_recv()
+        far_x[d][1].wait_recv()
+        view = queries.at[:, turn(z, d), :, my_part]
+        return send(view, view, dc=1)
+
+    out_copies, stay = [], []
+
+    def score(d, from_core):
+        to = turn(z, d)
+        from_core.wait_recv()
+
+        @pl.loop(0, RING)
+        def _(k):
+            value = lax.dot_general(
+                trains[k], queries[k, to], (((1,), (1,)), ((), ())), preferred_element_type=jnp.float32
+            )
+
+            @pl.when(k == 0)
+            def _():
+                product[...] = value
+
+            @pl.when(k > 0)
+            def _():
+                product[...] += value
+
+        value = product[...]
+        top = jnp.maximum(jnp.max(jnp.abs(value), axis=1, keepdims=True), 1e-30)
+        ready[d] = jnp.round(value * (TOP / top)).astype(jnp.int32).astype(jnp.int16)
+        ready_scale[d] = jnp.transpose(jnp.broadcast_to(top * (1.0 / TOP), (rows, 128)))[:8]
+        if d == 0:
+            stay.append(pltpu.make_async_copy(ready.at[0], out_ref.at[z], own_sem.at[2]))
+            stay.append(pltpu.make_async_copy(ready_scale.at[0], out_scale_ref.at[z], own_sem.at[3]))
+            for copy in stay:
+                copy.start()
+            return
+        out_copies.append(send(ready_scale.at[d], out_scale_ref.at[z], dz=d))
+        for h in range(2):
+            part = pl.ds(h * half, half)
+            out_copies.append(send(ready.at[d, part], out_ref.at[z, part], dz=d))
+
+    from_core = {0: complete(0)}
     far_x[3] = relay_x(3)
-    far_x[1] = relay_x(1)
     slot_round(3)
     near_y[1, 1].wait_recv()
     near_y[3, 0].wait_recv()
     far_y[0].wait_recv()
     far_y[1].wait_recv()
-
-    def multiply(at_x, first=False):
-        from_core[at_x].wait_recv()
-        place = turn(x, at_x)
-
-        @pl.loop(0, RING)
-        def _(to):
-            value = lax.dot_general(
-                trains[place], queries[place, to], (((1,), (1,)), ((), ())), preferred_element_type=jnp.float32
-            )
-            if first:
-                products[to] = value
-            else:
-                products[to] += value
-
-    multiply(0, True)
+    score(0, from_core[0])
+    from_core[3] = complete(3)
+    far_x[1] = relay_x(1)
+    score(3, from_core[3])
+    from_core[1] = complete(1)
     far_x[2] = relay_x(2)
-    for d in range(RING):
-        along_x[d][1, 1].wait_recv()
-        along_x[d][3, 0].wait_recv()
-    from_core[3] = to_core(turn(x, 3))
-    from_core[1] = to_core(turn(x, 1))
-    multiply(3)
-    multiply(1)
-    for d in range(RING):
-        far_x[d][0].wait_recv()
-        far_x[d][1].wait_recv()
-    from_core[2] = to_core(turn(x, 2))
-    multiply(2)
-
-    @pl.loop(0, RING)
-    def _(to):
-        value = products[to]
-        top = jnp.maximum(jnp.max(jnp.abs(value), axis=1, keepdims=True), 1e-30)
-        ready[to] = jnp.round(value * (TOP / top)).astype(jnp.int32).astype(jnp.int16)
-        ready_scale[to] = jnp.transpose(jnp.broadcast_to(top * (1.0 / TOP), (rows, 128)))[:8]
-
-    out_copies = []
-    for d in (1, 3, 2):
-        out_copies.append(send(ready_scale.at[turn(z, d)], out_scale_ref.at[z], dz=d))
-        for h in range(2):
-            part = pl.ds(h * half, half)
-            out_copies.append(send(ready.at[turn(z, d), part], out_ref.at[z, part], dz=d))
-    stay = [
-        pltpu.make_async_copy(ready.at[z], out_ref.at[z], own_sem.at[5]),
-        pltpu.make_async_copy(ready_scale.at[z], out_scale_ref.at[z], own_sem.at[6]),
-    ]
-    for copy in stay:
-        copy.start()
-
-    own[2].wait()
-    own[3].wait()
+    score(1, from_core[1])
+    from_core[2] = complete(2)
+    score(2, from_core[2])
+
     for copy in slot_copies:
         copy.wait_recv()
     step = 512
 
-    @pl.loop(0, parts.shape[1])
+    @pl.loop(0, pairs)
     def _(p):
-        slot = owner_ref[p]
+        slot = cand_ref[qry * (pairs // CANDS) + p // CANDS, p % CANDS] // held
         tile = p // CANDS
         total = jnp.zeros((BLOCK_ROWS, BLOCK_ROWS), jnp.float32)
         for c in range(0, width, step):
@@ -296,17 +302,10 @@
 
 def local(train_proj, query_proj, out_weight, train_feat, query_feat, candidates):
     n_qry, n_ex = lax.axis_size("qry"), lax.axis_size("ex")
-    my_index = lax.axis_index("qry")
     width = train_feat.shape[1]
     held_blocks = train_feat.shape[0] // BLOCK_ROWS
     tiles_here = query_feat.shape[0] // BLOCK_ROWS
     pairs = tiles_here * CANDS
-    items = candidates.reshape(n_qry, pairs)
-    wanted_here = items // held_blocks == my_index
-    pick = jnp.sum(jnp.where(wanted_here, items % held_blocks, 0), axis=1)
-    my_owner = lax.dynamic_slice_in_dim(items, my_index, 1, 0)[0] // held_blocks
-    codes, scale = code_slots(pick, train_feat)
-
     depth = train_proj.shape[1]
     rows = train_proj.shape[0] // RING
     columns, part_depth = query_proj.shape
@@ -320,35 +319,40 @@
             jax.ShapeDtypeStruct((RING, 8, rows), jnp.float32),
             jax.ShapeDtypeStruct((pairs, share, BLOCK_ROWS), jnp.float32),
         ],
-        in_specs=[pl.BlockSpec(memory_space=pltpu.SMEM)] + [any_space] * 5,
-        out_specs=[vmem, vmem, vmem],
+        in_specs=[pl.BlockSpec(memory_space=pltpu.SMEM)] + [any_space] * 4,
+        out_specs=[any_space, any_space, vmem],
         scratch_shapes=[
+            pltpu.SMEM((n_qry,), jnp.int32),
+            pltpu.VMEM((tiles_here, BLOCK_ROWS, width), jnp.float32),
+            pltpu.VMEM((held_blocks, BLOCK_ROWS, width), jnp.int16),
+            pltpu.VMEM((held_blocks, 8, BLOCK_ROWS), jnp.float32),
+            pltpu.VMEM((n_qry, BLOCK_ROWS, width), jnp.int16),
+            pltpu.VMEM((n_qry, 8, BLOCK_ROWS), jnp.float32),
             pltpu.VMEM((RING, rows, RING * depth), jnp.bfloat16),
             pltpu.VMEM((RING, RING, columns, 2 * part_depth), jnp.bfloat16),
             pltpu.VMEM((n_qry, BLOCK_ROWS, width), jnp.int16),
             pltpu.VMEM((n_qry, 8, BLOCK_ROWS), jnp.float32),
-            pltpu.VMEM((tiles_here, BLOCK_ROWS, width), jnp.float32),
             pltpu.VMEM((2, tiles_here, BLOCK_ROWS, width), jnp.bfloat16),
-            pltpu.VMEM((RING, rows, columns), jnp.float32),
+            pltpu.VMEM((rows, columns), jnp.float32),
             pltpu.VMEM((RING, rows, columns), jnp.int16),
             pltpu.VMEM((RING, 8, rows), jnp.float32),
             pltpu.VMEM((n_ex, pairs, share, BLOCK_ROWS), jnp.float32),
             pltpu.VMEM((n_ex, pairs, share, BLOCK_ROWS), jnp.float32),
-            dma((8,)),
+            dma((tiles_here,)),
+            dma((4,)),
             dma((COPIES,)),
             dma((COPIES,)),
         ],
         compiler_params=pltpu.CompilerParams(
-            collective_id=0, has_side_effects=True, vmem_limit_bytes=58 * MIB
+            collective_id=0, has_side_effects=True, vmem_limit_bytes=61 * MIB
         ),
         name="main",
     )(
-        my_owner,
+        candidates,
         train_proj.reshape(RING, rows, depth),
         query_proj,
+        train_feat.reshape(held_blocks, BLOCK_ROWS, width),
         query_feat.reshape(tiles_here, BLOCK_ROWS, width),
-        codes,
-        scale,
     )
     scores = pl.pallas_call(
         decode_kernel,

time: 197 us -> 185 us (0.939)
  local copies, waits for them, and re-layouts: 11.2 us -> 4.44 us
  Pallas kernels: 184 us -> 180 us
    unnamed x16 -> x10, local copies, waits for them, and re-layouts: 11.1 us -> 4.44 us
    pallas_call x1 -> x0, Pallas kernels: 3.78 us -> none  [code_slots(): pl.pallas_call(code_kernel, grid_spec=pltpu.PrefetchScalarGridSpec(num_sc...]
where the time goes in v3:
time: 185 us
  Pallas kernels  180 us (97%)
  local copies, waits for them, and re-layouts  4.44 us (2%)
    pallas_call x1, Pallas kernels, local(): pl.pallas_call(main_kernel, out_shape=[jax.ShapeDtypeStruct((RING, rows,...  177 us
    unnamed x10, local copies, waits for them, and re-layouts  4.44 us

profile of v3, /device:TPU:9, one launch (start us, length us, event | category | flops | bytes accessed | tf_op | source)
XLA Modules:
  0.0 184.8 jit_solution(5588667502113539456)
XLA Ops:
  0.6 1.4 copy.8.cand_ref
  2.0 0.0 copy-start.2
  2.0 176.9 %main.1 = (s16[4,512,512]{2,1,0:T(8,128)(2,1)}, f32[4,8,512]{2,1,0:T(8,128)}, f32[8,16,128]{2,1,0:T(8,128)}) custom-call(s32[64,2]{1,0:T(8,128)} %copy.8.cand_ref, bf16[4,512,256]{2,1,0:T(8,128)(2,1)} %bitcast.8, bf16[512,512]{1,0:T(8,128)(2,1)} %query_ref.1, f32[8,128,2048]{2,1,0:T(8,128)} %bitcast.6, f32[4,128,2048]{2,1,0:T(8,128)} %bitcast.7), custom_call_target="tpu_custom_call" | custom-call | tf_op jit(solution)/shard_map/main/pallas_call | solution.py:315
  179.0 0.0 copy-done.2
  179.0 0.0 copy-start
  179.0 1.6 copy-done
  180.6 0.0 copy-start.1
  180.6 0.8 copy-done.1
  181.4 0.0 copy-start.3
  181.4 2.7 %decode.1 = f32[2048,512]{1,0:T(8,128)} custom-call(s16[4,512,512]{2,1,0:T(8,128)(2,1)S(1)} %copy-done, f32[4,8,512]{2,1,0:T(8,128)S(1)} %copy-done.1, f32[4,1,512]{2,1,0:T(1,128)S(1)} %bitcast.5), custom_call_target="tpu_custom_call" | custom-call | tf_op jit(solution)/shard_map/decode/pallas_call | solution.py:357
  184.2 0.0 copy-done.3
  184.2 0.6 copy.10
Async XLA Ops:
  2.0 177.0 %copy-start.2 = (f32[2048]{0:T(1024)S(1)}, f32[2048]{0:T(1024)}, u32[]{:S(2)}) copy-start(f32[2048]{0:T(1024)} %param.8) | copy-start | bytes 24580
  179.0 1.6 copy-start
  180.6 0.8 copy-start.1
  181.4 2.8 %copy-start.3 = (f32[8,16,128]{2,1,0:T(8,128)S(1)}, f32[8,16,128]{2,1,0:T(8,128)}, u32[]{:S(2)}) copy-start(f32[8,16,128]{2,1,0:T(8,128)} %get-tuple-element.7) | copy-start | bytes 196612

commit v4 on v3

--- a/solution.py
+++ b/solution.py
@@ -8,8 +8,8 @@
 BLOCK_ROWS = 128
 CANDS = 2
 RING = 4
-SLOT_CHUNKS = 4
-COPIES = 144
+SLOT_CHUNKS = 2
+COPIES = 136
 TOP = 32752.0
 MESH = pl.DeviceIdType.MESH
 MIB = 1 << 20
@@ -18,12 +18,13 @@
 def main_kernel(
     cand_ref, train_ref, query_ref, blocks_ref, tiles_ref,
     out_ref, out_scale_ref, exact_ref,
-    pick, stage, coded, coded_scale, leaving, leaving_scale,
-    trains, queries, slots, slot_scale, split, product, ready, ready_scale, parts, parts_in,
+    pick, pair_block, pair_tile, stage, coded, coded_scale, tile0, tile1, tile2, tile3, tile_scale,
+    block_scales, tile_scales, leaving, slots, trains, queries, product, ready, ready_scale,
+    parts, parts_in, back, back_in,
     stage_sem, own_sem, send_sem, recv_sem,
 ):
     ex, qry = lax.axis_index("ex"), lax.axis_index("qry")
-    n_ex, n_qry = parts.shape[0], slots.shape[0]
+    n_ex, n_qry = parts.shape[1], RING * RING
     x, core, y, z = ex // 2, ex % 2, qry // RING, qry % RING
     turn = lambda a, d: (a + d) % RING
     sent = []
@@ -43,7 +44,7 @@
         sent.append(copy)
         return copy
 
-    rows, width = trains.shape[1], slots.shape[2]
+    rows, width = trains.shape[1], slots.shape[3]
     depth, part_depth = train_ref.shape[2], query_ref.shape[1]
     half = rows // 2
     my_depth = pl.ds(pl.multiple_of(z * depth, depth), depth)
@@ -91,60 +92,72 @@
         send(train_ref.at[turn(z, d)], trains.at[y, :, my_depth], dz=d) for d in (1, 3, 2)
     ]
 
-    held = coded.shape[0]
-    pairs = parts.shape[1]
+    held, n_tiles = coded.shape[0], tile0.shape[0]
+    pairs = n_tiles * CANDS
 
     def wanted(q, p):
-        return cand_ref[q * (pairs // CANDS) + p // CANDS, p % CANDS]
+        return cand_ref[q * n_tiles + p // CANDS, p % CANDS]
 
     @pl.loop(0, n_qry)
-    def _(q):
-        block = jnp.int32(0)
+    def _(i):
+        row, ring = i % RING, turn(z, i // RING)
+        here, block, tile = jnp.int32(0), jnp.int32(0), jnp.int32(0)
         for p in range(pairs):
-            item = wanted(q, p)
-            block += jnp.where(item // held == qry, item % held, 0)
-        pick[q] = block
-
-    def code(b):
+            place = wanted(row * RING + ring, p) - qry * held
+            here = jnp.where((place >= 0) & (place < held), place, here)
+            place = wanted(y * RING + ring, p) - (row * RING + z) * held
+            match = (place >= 0) & (place < held)
+            block = jnp.where(match, place, block)
+            tile = jnp.where(match, p // CANDS, tile)
+        pick[i] = here
+        pair_block[i] = block
+        pair_tile[i] = tile
+
+    def code(place, to, at, line_to):
+        whole = stage[place]
+        top = jnp.maximum(jnp.max(jnp.abs(whole), axis=1, keepdims=True), 1e-30)
+        to[at] = jnp.round(whole * (TOP / top)).astype(jnp.int32).astype(jnp.int16)
+        wide = jnp.broadcast_to(top * (1.0 / TOP), (BLOCK_ROWS, BLOCK_ROWS))
+        line_to[pl.ds(at, 1)] = jnp.transpose(wide)[:1].reshape(1, 1, BLOCK_ROWS)
+
+    for b in range(held):
         place = b % depth_of_stage
         fetch(blocks_ref, b, place).wait()
-        whole = stage[place]
-        top = jnp.maximum(jnp.max(jnp.abs(whole), axis=1, keepdims=True), 1e-30)
-        coded[b] = jnp.round(whole * (TOP / top)).astype(jnp.int32).astype(jnp.int16)
-        wide = jnp.broadcast_to(top * (1.0 / TOP), (BLOCK_ROWS, BLOCK_ROWS))
-        coded_scale[b] = jnp.transpose(wide)[:8]
-
-    @pl.loop(0, depth_of_stage)
-    def _(b):
-        code(b)
-        fetch(blocks_ref, b + depth_of_stage, b).start()
-
-    @pl.loop(depth_of_stage, held)
-    def _(b):
-        code(b)
-        fetch(tiles_ref, b - depth_of_stage, b - depth_of_stage).start()
-
-    @pl.loop(0, n_qry)
-    def _(q):
-        leaving[q] = coded[pick[q]]
-        leaving_scale[q] = coded_scale[pick[q]]
-
-    slots[qry] = coded[pick[qry]]
-    slot_scale[qry] = coded_scale[pick[qry]]
-
-    slot_copies = []
-    order = ((0, 1), (1, 0), (0, 3), (3, 0), (1, 1), (3, 3), (1, 3), (3, 1), (2, 1), (1, 2), (2, 3), (3, 2), (0, 2), (2, 0), (2, 2))
+        code(place, coded, b, coded_scale)
+        if b + depth_of_stage < held:
+            fetch(blocks_ref, b + depth_of_stage, place).start()
+        else:
+            fetch(tiles_ref, b + depth_of_stage - held, place).start()
+
+    block_scales[y] = coded_scale[...]
+    slot_copies = {d: [] for d in range(RING)}
+    for d in range(1, RING):
+        slot_copies[0].append(send(coded_scale, block_scales.at[y], dy=d))
     chunk = BLOCK_ROWS // SLOT_CHUNKS
 
-    def slot_round(r):
-        for dy, dz in order:
-            there = turn(y, dy) * RING + turn(z, dz)
-            if r == 0:
-                slot_copies.append(send(leaving_scale.at[there], slot_scale.at[qry], dy=dy, dz=dz))
+    def slot_group(d):
+        slots[y, d] = coded[pick[d * RING + y]]
+        for dy in range(1, RING):
+            leaving[dy - 1, d] = coded[pick[d * RING + turn(y, dy)]]
+        for r in range(SLOT_CHUNKS):
             part = pl.ds(r * chunk, chunk)
-            slot_copies.append(send(leaving.at[there, part], slots.at[qry, part], dy=dy, dz=dz))
-
-    slot_round(0)
+            for dy in (1, 3, 2):
+                slot_copies[d].append(send(leaving.at[dy - 1, d, part], slots.at[y, d, part], dy=dy))
+
+    slot_group(0)
+
+    tile_at = [tile0, tile1, tile2, tile3]
+    for t in range(n_tiles):
+        fetch(tiles_ref, t, t).wait()
+        code(t, tile0, t, tile_scale)
+    tile_scales[0] = tile_scale[...]
+    scale_copies = [send(tile_scale, tile_scales.at[RING - d], dz=d) for d in range(1, RING)]
+
+    near_tile = {}
+    for k in range(n_tiles):
+        near_tile[1, k] = send(tile0.at[k], tile3.at[k], dz=1)
+        k = n_tiles - 1 - k
+        near_tile[3, k] = send(tile0.at[k], tile1.at[k], dz=3)
 
     near_z[1, 0].wait_recv()
     far_z = {0: send(query_half(x, turn(z, 3), 0), query_half(x, turn(z, 3), 0), dz=1)}
@@ -166,7 +179,7 @@
     for h in range(2):
         for d in (1, 3):
             near_y[d, h] = send(train_half(y, h), train_half(y, h), dy=d)
-    slot_round(1)
+    slot_group(3)
 
     def relay_x(d):
         at_z = turn(z, d)
@@ -185,15 +198,16 @@
     far_y = {0: send(train_half(turn(y, 3), 0), train_half(turn(y, 3), 0), dy=1)}
     near_y[3, 1].wait_recv()
     far_y[1] = send(train_half(turn(y, 1), 1), train_half(turn(y, 1), 1), dy=3)
-    slot_round(2)
-
-    @pl.loop(0, split.shape[1])
-    def _(t):
-        fetch(tiles_ref, t, t).wait()
-        whole = stage[t]
-        high = whole.astype(jnp.bfloat16)
-        split[0, t] = high
-        split[1, t] = (whole - high.astype(jnp.float32)).astype(jnp.bfloat16)
+    slot_group(1)
+
+    far_tile = []
+    for k in range(n_tiles // 2):
+        near_tile[1, k].wait_recv()
+        far_tile.append(send(tile3.at[k], tile2.at[k], dz=1))
+        k = n_tiles - 1 - k
+        near_tile[3, k].wait_recv()
+        far_tile.append(send(tile1.at[k], tile2.at[k], dz=3))
+    slot_group(2)
 
     own[1].wait()
 
@@ -240,14 +254,70 @@
             part = pl.ds(h * half, half)
             out_copies.append(send(ready.at[d, part], out_ref.at[z, part], dz=d))
 
+    step = 512
+
+    def halves(codes):
+        value = codes.astype(jnp.float32)
+        high = value.astype(jnp.bfloat16)
+        return high, (value - high.astype(jnp.float32)).astype(jnp.bfloat16)
+
+    def line_of(lines, index):
+        row = lax.broadcasted_iota(jnp.int32, lines.shape, 0)
+        return jnp.sum(jnp.where(row == index, lines, 0.0), axis=0, keepdims=True)
+
+    part_copies, back_copies = {}, []
+
+    def exact_dots(d):
+        if d in (1, 3):
+            for k in range(n_tiles // 2):
+                k = k if d == 1 else n_tiles - 1 - k
+                near_tile[RING - d, k].wait_recv()
+        if d == 2:
+            for copy in far_tile:
+                copy.wait_recv()
+        for copy in slot_copies[d]:
+            copy.wait_recv()
+
+        @pl.loop(0, RING)
+        def _(j):
+            block, tile = pair_block[d * RING + j], pair_tile[d * RING + j]
+            total = jnp.zeros((BLOCK_ROWS, BLOCK_ROWS), jnp.float32)
+            for c in range(0, width, step):
+                high, low = halves(slots[j, d, :, c : c + step])
+                tile_high, tile_low = halves(tile_at[d][tile, :, c : c + step])
+                for a, b in ((high, tile_high), (high, tile_low), (low, tile_high)):
+                    total += lax.dot_general(a, b, (((1,), (1,)), ((), ())), preferred_element_type=jnp.float32)
+            line = line_of(block_scales[j, :, 0], block)
+            tall = jnp.transpose(jnp.broadcast_to(line, (BLOCK_ROWS, BLOCK_ROWS)))
+            total = total * tall * line_of(tile_scales[d, :, 0], tile)
+            parts[d, :, j] = total.reshape(n_ex, parts.shape[3], BLOCK_ROWS)
+
+        part_copies[d] = []
+        for k in range(1, n_ex):
+            there = turn(x, k // 2) * 2 + (core + k % 2) % 2
+            part_copies[d].append(send(parts.at[d, there], parts_in.at[d, k], dx=k // 2, dc=k % 2))
+
+    def exact_sum(d):
+        total = parts[d, ex]
+        for k, copy in enumerate(part_copies[d], 1):
+            copy.wait_recv()
+            total += parts_in[d, k]
+        if d == 0:
+            back_in[z] = total
+        else:
+            back[d] = total
+            back_copies.append(send(back.at[d], back_in.at[z], dz=d))
+
     from_core = {0: complete(0)}
     far_x[3] = relay_x(3)
-    slot_round(3)
     near_y[1, 1].wait_recv()
     near_y[3, 0].wait_recv()
     far_y[0].wait_recv()
     far_y[1].wait_recv()
     score(0, from_core[0])
+    for copy in scale_copies:
+        copy.wait_recv()
+    exact_dots(0)
     from_core[3] = complete(3)
     far_x[1] = relay_x(1)
     score(3, from_core[3])
@@ -256,35 +326,19 @@
     score(1, from_core[1])
     from_core[2] = complete(2)
     score(2, from_core[2])
-
-    for copy in slot_copies:
+    exact_dots(3)
+    exact_sum(0)
+    exact_dots(1)
+    exact_sum(3)
+    exact_dots(2)
+
+    exact_sum(1)
+    exact_sum(2)
+    for copy in back_copies:
         copy.wait_recv()
-    step = 512
-
-    @pl.loop(0, pairs)
-    def _(p):
-        slot = cand_ref[qry * (pairs // CANDS) + p // CANDS, p % CANDS] // held
-        tile = p // CANDS
-        total = jnp.zeros((BLOCK_ROWS, BLOCK_ROWS), jnp.float32)
-        for c in range(0, width, step):
-            block = slots[slot, :, c : c + step].astype(jnp.float32)
-            high = block.astype(jnp.bfloat16)
-            low = (block - high.astype(jnp.float32)).astype(jnp.bfloat16)
-            tile_high, tile_low = split[0, tile, :, c : c + step], split[1, tile, :, c : c + step]
-            for a, b in ((high, tile_high), (high, tile_low), (low, tile_high)):
-                total += lax.dot_general(a, b, (((1,), (1,)), ((), ())), preferred_element_type=jnp.float32)
-        tall = jnp.transpose(jnp.broadcast_to(slot_scale[slot][:1], (BLOCK_ROWS, BLOCK_ROWS)))
-        parts[:, p] = (total * tall).reshape(parts.shape[0], parts.shape[2], BLOCK_ROWS)
-
-    part_copies = []
-    for d in range(1, n_ex):
-        there = turn(x, d // 2) * 2 + (core + d % 2) % 2
-        part_copies.append(send(parts.at[there], parts_in.at[d], dx=d // 2, dc=d % 2))
-    total = parts[ex]
-    for d, copy in enumerate(part_copies, 1):
-        copy.wait_recv()
-        total += parts_in[d]
-    exact_ref[...] = total
+    for p in range(pairs):
+        owner = wanted(qry, p) // held
+        exact_ref[p] = back_in[owner % RING, owner // RING]
 
     for copy in out_copies:
         copy.wait_recv()
@@ -323,21 +377,29 @@
         out_specs=[any_space, any_space, vmem],
         scratch_shapes=[
             pltpu.SMEM((n_qry,), jnp.int32),
+            pltpu.SMEM((n_qry,), jnp.int32),
+            pltpu.SMEM((n_qry,), jnp.int32),
             pltpu.VMEM((tiles_here, BLOCK_ROWS, width), jnp.float32),
             pltpu.VMEM((held_blocks, BLOCK_ROWS, width), jnp.int16),
-            pltpu.VMEM((held_blocks, 8, BLOCK_ROWS), jnp.float32),
-            pltpu.VMEM((n_qry, BLOCK_ROWS, width), jnp.int16),
-            pltpu.VMEM((n_qry, 8, BLOCK_ROWS), jnp.float32),
+            pltpu.VMEM((held_blocks, 1, BLOCK_ROWS), jnp.float32),
+            pltpu.VMEM((tiles_here, BLOCK_ROWS, width), jnp.int16),
+            pltpu.VMEM((tiles_here, BLOCK_ROWS, width), jnp.int16),
+            pltpu.VMEM((tiles_here, BLOCK_ROWS, width), jnp.int16),
+            pltpu.VMEM((tiles_here, BLOCK_ROWS, width), jnp.int16),
+            pltpu.VMEM((tiles_here, 1, BLOCK_ROWS), jnp.float32),
+            pltpu.VMEM((RING, held_blocks, 1, BLOCK_ROWS), jnp.float32),
+            pltpu.VMEM((RING, tiles_here, 1, BLOCK_ROWS), jnp.float32),
+            pltpu.VMEM((RING - 1, RING, BLOCK_ROWS, width), jnp.int16),
+            pltpu.VMEM((RING, RING, BLOCK_ROWS, width), jnp.int16),
             pltpu.VMEM((RING, rows, RING * depth), jnp.bfloat16),
             pltpu.VMEM((RING, RING, columns, 2 * part_depth), jnp.bfloat16),
-            pltpu.VMEM((n_qry, BLOCK_ROWS, width), jnp.int16),
-            pltpu.VMEM((n_qry, 8, BLOCK_ROWS), jnp.float32),
-            pltpu.VMEM((2, tiles_here, BLOCK_ROWS, width), jnp.bfloat16),
             pltpu.VMEM((rows, columns), jnp.float32),
             pltpu.VMEM((RING, rows, columns), jnp.int16),
             pltpu.VMEM((RING, 8, rows), jnp.float32),
-            pltpu.VMEM((n_ex, pairs, share, BLOCK_ROWS), jnp.float32),
-            pltpu.VMEM((n_ex, pairs, share, BLOCK_ROWS), jnp.float32),
+            pltpu.VMEM((RING, n_ex, RING, share, BLOCK_ROWS), jnp.float32),
+            pltpu.VMEM((RING, n_ex, RING, share, BLOCK_ROWS), jnp.float32),
+            pltpu.VMEM((RING, RING, share, BLOCK_ROWS), jnp.float32),
+            pltpu.VMEM((RING, RING, share, BLOCK_ROWS), jnp.float32),
             dma((tiles_here,)),
             dma((4,)),
             dma((COPIES,)),

time: 185 us -> 165 us (0.89); the launches traced: 185 us -> 163 us
  Pallas kernels: 180 us -> 157 us
    pallas_call x1, Pallas kernels: 177 us -> 155 us  [local(): pl.pallas_call(main_kernel, out_shape=[jax.ShapeDtypeStruct((RING, rows,...]
where the time goes in v4:
time: 165 us; the launch traced here: 163 us
  Pallas kernels  157 us (95%)
  local copies, waits for them, and re-layouts  4.44 us (3%)
    pallas_call x1, Pallas kernels, local(): pl.pallas_call(main_kernel, out_shape=[jax.ShapeDtypeStruct((RING, rows,...  155 us
    unnamed x10, local copies, waits for them, and re-layouts  4.44 us

profile of v4, /device:TPU:9, one launch (start us, length us, event | category | flops | bytes accessed | tf_op | source)
XLA Modules:
  0.0 162.5 jit_solution(13132333544558623341)
XLA Ops:
  0.6 1.4 copy.8.cand_ref
  2.0 0.0 copy-start.2
  2.0 154.7 %main.1 = (s16[4,512,512]{2,1,0:T(8,128)(2,1)}, f32[4,8,512]{2,1,0:T(8,128)}, f32[8,16,128]{2,1,0:T(8,128)}) custom-call(s32[64,2]{1,0:T(8,128)} %copy.8.cand_ref, bf16[4,512,256]{2,1,0:T(8,128)(2,1)} %bitcast.8, bf16[512,512]{1,0:T(8,128)(2,1)} %query_ref.1, f32[8,128,2048]{2,1,0:T(8,128)} %bitcast.6, f32[4,128,2048]{2,1,0:T(8,128)} %bitcast.7), custom_call_target="tpu_custom_call" | custom-call | tf_op jit(solution)/shard_map/main/pallas_call | solution.py:369
  156.7 0.0 copy-done.2
  156.7 0.0 copy-start
  156.7 1.6 copy-done
  158.3 0.0 copy-start.1
  158.3 0.8 copy-done.1
  159.1 0.0 copy-start.3
  159.1 2.7 %decode.1 = f32[2048,512]{1,0:T(8,128)} custom-call(s16[4,512,512]{2,1,0:T(8,128)(2,1)S(1)} %copy-done, f32[4,8,512]{2,1,0:T(8,128)S(1)} %copy-done.1, f32[4,1,512]{2,1,0:T(1,128)S(1)} %bitcast.5), custom_call_target="tpu_custom_call" | custom-call | tf_op jit(solution)/shard_map/decode/pallas_call | solution.py:419
  161.9 0.0 copy-done.3
  161.9 0.6 copy.10
Async XLA Ops:
  2.0 154.7 %copy-start.2 = (f32[2048]{0:T(1024)S(1)}, f32[2048]{0:T(1024)}, u32[]{:S(2)}) copy-start(f32[2048]{0:T(1024)} %param.8) | copy-start | bytes 24580
  156.7 1.6 copy-start
  158.3 0.8 copy-start.1
  159.1 2.8 %copy-start.3 = (f32[8,16,128]{2,1,0:T(8,128)S(1)}, f32[8,16,128]{2,1,0:T(8,128)}, u32[]{:S(2)}) copy-start(f32[8,16,128]{2,1,0:T(8,128)} %get-tuple-element.7) | copy-start | bytes 196612

commit v5 on v4

--- a/solution.py
+++ b/solution.py
@@ -92,6 +92,24 @@
         send(train_ref.at[turn(z, d)], trains.at[y, :, my_depth], dz=d) for d in (1, 3, 2)
     ]
 
+    near_y, far_y = {}, {}
+
+    def train_part(at_y, d, first=0, many=None):
+        columns = pl.ds(pl.multiple_of(turn(z, d) * depth, depth), depth)
+        return trains.at[at_y, pl.ds(first, many or rows), columns]
+
+    def train_sends(d, source):
+        for dy in (1, 3):
+            near_y[d, dy] = send(source, train_part(y, d), dy=dy)
+
+    def train_relay(d):
+        for dy, first in ((1, 0), (3, half)):
+            near_y[d, dy].wait_recv()
+            view = train_part(turn(y, RING - dy), d, first, half)
+            far_y[d, dy] = send(view, view, dy=dy)
+
+    train_sends(0, train_ref.at[z])
+
     held, n_tiles = coded.shape[0], tile0.shape[0]
     pairs = n_tiles * CANDS
 
@@ -153,12 +171,6 @@
     tile_scales[0] = tile_scale[...]
     scale_copies = [send(tile_scale, tile_scales.at[RING - d], dz=d) for d in range(1, RING)]
 
-    near_tile = {}
-    for k in range(n_tiles):
-        near_tile[1, k] = send(tile0.at[k], tile3.at[k], dz=1)
-        k = n_tiles - 1 - k
-        near_tile[3, k] = send(tile0.at[k], tile1.at[k], dz=3)
-
     near_z[1, 0].wait_recv()
     far_z = {0: send(query_half(x, turn(z, 3), 0), query_half(x, turn(z, 3), 0), dz=1)}
     near_z[3, 1].wait_recv()
@@ -168,17 +180,16 @@
     near_z[3, 0].wait_recv()
     along_x[1] = query_sends(lambda h: query_half(x, turn(z, 1), h), turn(z, 1))
 
-    for copy in train_z:
+    train_relay(0)
+    for d, copy in zip((3, 1, 2), train_z):
         copy.wait_recv()
-    own[0].wait()
-
-    def train_half(at_y, h):
-        return trains.at[at_y, pl.ds(h * half, half)]
-
-    near_y = {}
-    for h in range(2):
-        for d in (1, 3):
-            near_y[d, h] = send(train_half(y, h), train_half(y, h), dy=d)
+        train_sends(d, train_part(y, d))
+    near_tile = {}
+    for k in range(n_tiles):
+        near_tile[1, k] = send(tile0.at[k], tile3.at[k], dz=1)
+        k = n_tiles - 1 - k
+        near_tile[3, k] = send(tile0.at[k], tile1.at[k], dz=3)
+
     slot_group(3)
 
     def relay_x(d):
@@ -194,10 +205,8 @@
     far_z[0].wait_recv()
     far_z[1].wait_recv()
     along_x[2] = query_sends(lambda h: query_half(x, turn(z, 2), h), turn(z, 2))
-    near_y[1, 0].wait_recv()
-    far_y = {0: send(train_half(turn(y, 3), 0), train_half(turn(y, 3), 0), dy=1)}
-    near_y[3, 1].wait_recv()
-    far_y[1] = send(train_half(turn(y, 1), 1), train_half(turn(y, 1), 1), dy=3)
+    for d in (3, 1, 2):
+        train_relay(d)
     slot_group(1)
 
     far_tile = []
@@ -310,10 +319,9 @@
 
     from_core = {0: complete(0)}
     far_x[3] = relay_x(3)
-    near_y[1, 1].wait_recv()
-    near_y[3, 0].wait_recv()
-    far_y[0].wait_recv()
-    far_y[1].wait_recv()
+    own[0].wait()
+    for copy in far_y.values():
+        copy.wait_recv()
     score(0, from_core[0])
     for copy in scale_copies:
         copy.wait_recv()
@@ -330,9 +338,9 @@
     exact_sum(0)
     exact_dots(1)
     exact_sum(3)
+    exact_sum(1)
     exact_dots(2)
 
-    exact_sum(1)
     exact_sum(2)
     for copy in back_copies:
         copy.wait_recv()
@@ -426,7 +434,7 @@
         ],
         out_specs=pl.BlockSpec((rows, columns), lambda i: (i, 0)),
         out_shape=jax.ShapeDtypeStruct((RING * rows, columns), jnp.float32),
-        compiler_params=pltpu.CompilerParams(vmem_limit_bytes=24 * MIB),
+        compiler_params=pltpu.CompilerParams(vmem_limit_bytes=60 * MIB),
         name="decode",
     )(result, result_scale, out_weight.reshape(RING, 1, rows))
     return scores, exact.reshape(tiles_here, CANDS, share, BLOCK_ROWS)

time: 165 us -> 157 us (0.952)
  Pallas kernels: 157 us -> 152 us
  local copies, waits for them, and re-layouts: 4.44 us -> 2.02 us
    pallas_call x1, Pallas kernels: 155 us -> 147 us  [local(): pl.pallas_call(main_kernel, out_shape=[jax.ShapeDtypeStruct((RING, rows,...]
    unnamed x10 -> x4, local copies, waits for them, and re-layouts: 4.44 us -> 2.02 us
    pallas_call x1, Pallas kernels: 2.75 us -> 4.6 us  [local(): pl.pallas_call(decode_kernel, grid=(RING,), in_specs=[pl.BlockSpec((1, ro...]
where the time goes in v5:
time: 157 us; the launch traced here: 155 us
  Pallas kernels  152 us (97%)
  local copies, waits for them, and re-layouts  2.02 us (1%)
    pallas_call x1, Pallas kernels, local(): pl.pallas_call(main_kernel, out_shape=[jax.ShapeDtypeStruct((RING, rows,...  147 us
    pallas_call x1, Pallas kernels, local(): pl.pallas_call(decode_kernel, grid=(RING,), in_specs=[pl.BlockSpec((1, ro...  4.6 us

profile of v5, /device:TPU:9, one launch (start us, length us, event | category | flops | bytes accessed | tf_op | source)
XLA Modules:
  0.0 154.7 jit_solution(13389398172919471458)
XLA Ops:
  0.6 1.4 copy.8.cand_ref
  2.0 147.5 %main.1 = (s16[4,512,512]{2,1,0:T(8,128)(2,1)}, f32[4,8,512]{2,1,0:T(8,128)}, f32[8,16,128]{2,1,0:T(8,128)}) custom-call(s32[64,2]{1,0:T(8,128)} %copy.8.cand_ref, bf16[4,512,256]{2,1,0:T(8,128)(2,1)} %bitcast.7, bf16[512,512]{1,0:T(8,128)(2,1)} %query_ref.1, f32[8,128,2048]{2,1,0:T(8,128)} %bitcast.5, f32[4,128,2048]{2,1,0:T(8,128)} %bitcast.6), custom_call_target="tpu_custom_call" | custom-call | tf_op jit(solution)/shard_map/main/pallas_call | solution.py:377
  149.5 0.0 copy-start
  149.5 4.6 %decode.1 = f32[2048,512]{1,0:T(8,128)} custom-call(s16[4,512,512]{2,1,0:T(8,128)(2,1)} %get-tuple-element.5.codes_ref, f32[4,8,512]{2,1,0:T(8,128)} %get-tuple-element.6.scale_ref, f32[4,1,512]{2,1,0:T(1,128)} %bitcast.9), custom_call_target="tpu_custom_call" | custom-call | tf_op jit(solution)/shard_map/decode/pallas_call | solution.py:427
  154.1 0.0 copy-done
  154.1 0.6 copy.10
Async XLA Ops:
  149.5 4.6 %copy-start = (f32[8,16,128]{2,1,0:T(8,128)S(1)}, f32[8,16,128]{2,1,0:T(8,128)}, u32[]{:S(2)}) copy-start(f32[8,16,128]{2,1,0:T(8,128)} %get-tuple-element.7) | copy-start | bytes 196612

commit v6 on v5

--- a/solution.py
+++ b/solution.py
@@ -9,6 +9,7 @@
 CANDS = 2
 RING = 4
 SLOT_CHUNKS = 2
+MEMBERS = 2
 COPIES = 136
 TOP = 32752.0
 MESH = pl.DeviceIdType.MESH
@@ -16,9 +17,9 @@
 
 
 def main_kernel(
-    cand_ref, train_ref, query_ref, blocks_ref, tiles_ref,
+    cand_in_ref, train_ref, query_ref, blocks_ref, tiles_ref,
     out_ref, out_scale_ref, exact_ref,
-    pick, pair_block, pair_tile, stage, coded, coded_scale, tile0, tile1, tile2, tile3, tile_scale,
+    cand_ref, pick, pair_block, pair_tile, stage, coded, coded_scale, tile0, tile1, tile2, tile3, tile_scale,
     block_scales, tile_scales, leaving, slots, trains, queries, product, ready, ready_scale,
     parts, parts_in, back, back_in,
     stage_sem, own_sem, send_sem, recv_sem,
@@ -56,6 +57,8 @@
     ]
     for copy in own:
         copy.start()
+    cand_copy = pltpu.make_async_copy(cand_in_ref, cand_ref, own_sem.at[4])
+    cand_copy.start()
     depth_of_stage = stage.shape[0]
 
     def fetch(source, index, place):
@@ -83,15 +86,15 @@
                 out[d, h] = send(source(h), query_half(x, at_z, h), dx=d)
         return out
 
+    train_z = [
+        send(train_ref.at[turn(z, d)], trains.at[y, :, my_depth], dz=d) for d in (1, 3, 2)
+    ]
+
     near_z = {}
     for h in range(2):
         for d in (1, 3):
             near_z[d, h] = send(query_ref.at[pl.ds(h * half, half)], query_half(x, z, h), dz=d)
     along_x = {0: query_sends(lambda h: query_ref.at[pl.ds(h * half, half)], z)}
-    train_z = [
-        send(train_ref.at[turn(z, d)], trains.at[y, :, my_depth], dz=d) for d in (1, 3, 2)
-    ]
-
     near_y, far_y = {}, {}
 
     def train_part(at_y, d, first=0, many=None):
@@ -114,7 +117,9 @@
     pairs = n_tiles * CANDS
 
     def wanted(q, p):
-        return cand_ref[q * n_tiles + p // CANDS, p % CANDS]
+        return cand_ref[p % CANDS, q * n_tiles + p // CANDS]
+
+    cand_copy.wait()
 
     @pl.loop(0, n_qry)
     def _(i):
@@ -357,9 +362,11 @@
 
 
 def decode_kernel(codes_ref, scale_ref, weight_ref, scores_ref):
-    line = scale_ref[0][:1] * weight_ref[0]
-    tall = jnp.transpose(jnp.broadcast_to(line, (128, line.shape[1])))
-    scores_ref[...] = codes_ref[0].astype(jnp.float32) * tall[:, :1]
+    rows = codes_ref.shape[1]
+    for m in range(codes_ref.shape[0]):
+        line = scale_ref[m][:1] * weight_ref[m]
+        tall = jnp.transpose(jnp.broadcast_to(line, (128, rows)))
+        scores_ref[pl.ds(m * rows, rows)] = codes_ref[m].astype(jnp.float32) * tall[:, :1]
 
 
 def local(train_proj, query_proj, out_weight, train_feat, query_feat, candidates):
@@ -381,9 +388,10 @@
             jax.ShapeDtypeStruct((RING, 8, rows), jnp.float32),
             jax.ShapeDtypeStruct((pairs, share, BLOCK_ROWS), jnp.float32),
         ],
-        in_specs=[pl.BlockSpec(memory_space=pltpu.SMEM)] + [any_space] * 4,
+        in_specs=[any_space] * 5,
         out_specs=[any_space, any_space, vmem],
         scratch_shapes=[
+            pltpu.SMEM(candidates.shape[::-1], jnp.int32),
             pltpu.SMEM((n_qry,), jnp.int32),
             pltpu.SMEM((n_qry,), jnp.int32),
             pltpu.SMEM((n_qry,), jnp.int32),
@@ -409,7 +417,7 @@
             pltpu.VMEM((RING, RING, share, BLOCK_ROWS), jnp.float32),
             pltpu.VMEM((RING, RING, share, BLOCK_ROWS), jnp.float32),
             dma((tiles_here,)),
-            dma((4,)),
+            dma((5,)),
             dma((COPIES,)),
             dma((COPIES,)),
         ],
@@ -418,7 +426,7 @@
         ),
         name="main",
     )(
-        candidates,
+        candidates.T,
         train_proj.reshape(RING, rows, depth),
         query_proj,
         train_feat.reshape(held_blocks, BLOCK_ROWS, width),
@@ -426,13 +434,13 @@
     )
     scores = pl.pallas_call(
         decode_kernel,
-        grid=(RING,),
+        grid=(RING // MEMBERS,),
         in_specs=[
-            pl.BlockSpec((1, rows, columns), lambda i: (i, 0, 0)),
-            pl.BlockSpec((1, 8, rows), lambda i: (i, 0, 0)),
-            pl.BlockSpec((1, 1, rows), lambda i: (i, 0, 0)),
+            pl.BlockSpec((MEMBERS, rows, columns), lambda i: (i, 0, 0)),
+            pl.BlockSpec((MEMBERS, 8, rows), lambda i: (i, 0, 0)),
+            pl.BlockSpec((MEMBERS, 1, rows), lambda i: (i, 0, 0)),
         ],
-        out_specs=pl.BlockSpec((rows, columns), lambda i: (i, 0)),
+        out_specs=pl.BlockSpec((MEMBERS * rows, columns), lambda i: (i, 0)),
         out_shape=jax.ShapeDtypeStruct((RING * rows, columns), jnp.float32),
         compiler_params=pltpu.CompilerParams(vmem_limit_bytes=60 * MIB),
         name="decode",

time: 157 us -> 153 us (0.975)
  Pallas kernels: 152 us -> 150 us
where the time goes in v6:
time: 153 us; the launch traced here: 151 us
  Pallas kernels  150 us (98%)
    pallas_call x1, Pallas kernels, local(): pl.pallas_call(main_kernel, out_shape=[jax.ShapeDtypeStruct((RING, rows,...  146 us
    pallas_call x1, Pallas kernels, local(): pl.pallas_call(decode_kernel, grid=(RING // MEMBERS,), in_specs=[pl.Block...  3.7 us

profile of v6, /device:TPU:9, one launch (start us, length us, event | category | flops | bytes accessed | tf_op | source)
XLA Modules:
  0.0 151.3 jit_solution(5228976289850931821)
XLA Ops:
  0.6 146.3 %main.1 = (s16[4,512,512]{2,1,0:T(8,128)(2,1)}, f32[4,8,512]{2,1,0:T(8,128)}, f32[8,16,128]{2,1,0:T(8,128)}) custom-call(s32[2,64]{1,0:T(2,128)} %bitcast.11, bf16[4,512,256]{2,1,0:T(8,128)(2,1)} %bitcast.8, bf16[512,512]{1,0:T(8,128)(2,1)} %query_ref.1, f32[8,128,2048]{2,1,0:T(8,128)} %bitcast.6, f32[4,128,2048]{2,1,0:T(8,128)} %bitcast.7), custom_call_target="tpu_custom_call" | custom-call | tf_op jit(solution)/shard_map/main/pallas_call | solution.py:384
  147.0 0.0 copy-start
  147.0 3.7 %decode.1 = f32[2048,512]{1,0:T(8,128)} custom-call(s16[4,512,512]{2,1,0:T(8,128)(2,1)} %get-tuple-element.5.codes_ref, f32[4,8,512]{2,1,0:T(8,128)} %get-tuple-element.6.scale_ref, f32[4,1,512]{2,1,0:T(1,128)} %bitcast.10), custom_call_target="tpu_custom_call" | custom-call | tf_op jit(solution)/shard_map/decode/pallas_call | solution.py:435
  150.7 0.0 copy-done
  150.7 0.6 copy.9
Async XLA Ops:
  147.0 3.7 %copy-start = (f32[8,16,128]{2,1,0:T(8,128)S(1)}, f32[8,16,128]{2,1,0:T(8,128)}, u32[]{:S(2)}) copy-start(f32[8,16,128]{2,1,0:T(8,128)} %get-tuple-element.7) | copy-start | bytes 196612

commit v7 on v6

--- a/solution.py
+++ b/solution.py
@@ -8,7 +8,7 @@
 BLOCK_ROWS = 128
 CANDS = 2
 RING = 4
-SLOT_CHUNKS = 2
+SLOT_CHUNKS = 1
 MEMBERS = 2
 COPIES = 136
 TOP = 32752.0
@@ -214,6 +214,7 @@
         train_relay(d)
     slot_group(1)
 
+    slot_group(2)
     far_tile = []
     for k in range(n_tiles // 2):
         near_tile[1, k].wait_recv()
@@ -221,7 +222,6 @@
         k = n_tiles - 1 - k
         near_tile[3, k].wait_recv()
         far_tile.append(send(tile1.at[k], tile2.at[k], dz=3))
-    slot_group(2)
 
     own[1].wait()
 

time: 153 us -> 153 us (level)
  no operation moved by 1% of the time
where the time goes in v7:
time: 153 us; the launch traced here: 151 us
  Pallas kernels  150 us (98%)
    pallas_call x1, Pallas kernels, local(): pl.pallas_call(main_kernel, out_shape=[jax.ShapeDtypeStruct((RING, rows,...  146 us
    pallas_call x1, Pallas kernels, local(): pl.pallas_call(decode_kernel, grid=(RING // MEMBERS,), in_specs=[pl.Block...  3.7 us

profile of v7, /device:TPU:9, one launch (start us, length us, event | category | flops | bytes accessed | tf_op | source)
XLA Modules:
  0.0 151.1 jit_solution(15643169578129215397)
XLA Ops:
  0.6 146.1 %main.1 = (s16[4,512,512]{2,1,0:T(8,128)(2,1)}, f32[4,8,512]{2,1,0:T(8,128)}, f32[8,16,128]{2,1,0:T(8,128)}) custom-call(s32[2,64]{1,0:T(2,128)} %bitcast.11, bf16[4,512,256]{2,1,0:T(8,128)(2,1)} %bitcast.8, bf16[512,512]{1,0:T(8,128)(2,1)} %query_ref.1, f32[8,128,2048]{2,1,0:T(8,128)} %bitcast.6, f32[4,128,2048]{2,1,0:T(8,128)} %bitcast.7), custom_call_target="tpu_custom_call" | custom-call | tf_op jit(solution)/shard_map/main/pallas_call | solution.py:384
  146.8 0.0 copy-start
  146.8 3.7 %decode.1 = f32[2048,512]{1,0:T(8,128)} custom-call(s16[4,512,512]{2,1,0:T(8,128)(2,1)} %get-tuple-element.5.codes_ref, f32[4,8,512]{2,1,0:T(8,128)} %get-tuple-element.6.scale_ref, f32[4,1,512]{2,1,0:T(1,128)} %bitcast.10), custom_call_target="tpu_custom_call" | custom-call | tf_op jit(solution)/shard_map/decode/pallas_call | solution.py:435
  150.5 0.0 copy-done
  150.5 0.6 copy.9
Async XLA Ops:
  146.8 3.7 %copy-start = (f32[8,16,128]{2,1,0:T(8,128)S(1)}, f32[8,16,128]{2,1,0:T(8,128)}, u32[]{:S(2)}) copy-start(f32[8,16,128]{2,1,0:T(8,128)} %get-tuple-element.7) | copy-start | bytes 196612
